TPU v7x, 32 devices: a whole 2x2x4 slice. The times are simulated.
32 devices in a mesh: sec: 4 (over x, core), pts: 8 (over z, y).
Axes of the slice: x: 2, y: 2, z: 4, core: 2. Of those that a mesh axis runs over, the one named last changes fastest.
Arguments:
- points: bfloat16 [4, 8192, 1024], P('sec', 'pts'), may hold values from -10 to 10
- counts: int32 [4, 8], P('sec', 'pts'), may hold values from 256 to 1024, as said below
- input_gain: float32 [4, 1024], P('sec'), may hold values from 0.1 to 1.9
- key_weight: bfloat16 [4, 1024, 1024], P('sec', 'pts'), may hold values from -0.25 to 0.25
- value_weight: bfloat16 [4, 1024, 1024], P('sec', 'pts'), may hold values from -0.25 to 0.25
- query_weight: bfloat16 [1024, 1024], replicated, may hold values from -0.1875 to 0.1875
- output_weight: bfloat16 [1024, 1024], replicated, may hold values from -0.75 to 0.75
- middle_gain: float32 [1024], replicated, may hold values from 0.1 to 1.9
- up_weight: bfloat16 [1024, 4096], P(None, 'sec'), may hold values from -0.1875 to 0.1875
- down_weight: bfloat16 [4096, 1024], P('sec'), may hold values from -0.09375 to 0.09375
Outputs:
- updated: bfloat16 [8192, 1024], P('pts', 'sec')
Inputs may be any that keep to these rules, and one draw needn't show every extreme that they name: `counts`: each block has 1024 slots; in every section some block is full.
All inputs are finite; a program needn't handle non-finite values.
Results may differ from a plain program's by a relative error of at most 0.0049.
Values may be sent and summed in bfloat16 or wider, within the bound.
A program may use at most 128 MiB of HBM per device.

v0:
```python
import jax
import jax.numpy as jnp
from jax import lax
from jax.sharding import PartitionSpec as P

HEAD_DIM = 128


def broadcast(value, axis, root):
    mine = lax.axis_index(axis) == root
    return lax.psum(jnp.where(mine, value, jnp.zeros_like(value)), axis)


def layer_normalizer(values, gain):
    mean = jnp.mean(values, axis=-1, keepdims=True)
    centred = values - mean
    spread = jnp.mean(centred * centred, axis=-1, keepdims=True)
    return centred * lax.rsqrt(spread + 1e-05) * gain


def feature_map(values):
    return jax.nn.elu(values) + 1.0


def on_device(
    points,
    counts,
    input_gain,
    key_weight,
    value_weight,
    query_weight,
    output_weight,
    middle_gain,
    up_weight,
    down_weight,
):
    block = points[0]
    rows = block.shape[0]
    width = block.shape[1]
    heads = width // HEAD_DIM
    sections = lax.axis_size("sec")
    normed = layer_normalizer(block.astype(jnp.float32), input_gain[0]).astype(jnp.bfloat16)

    def add_rows(piece):
        return jnp.dot(normed, piece[0], preferred_element_type=jnp.float32)

    summed_keys = add_rows(lax.all_gather(key_weight, "pts", axis=1, tiled=True))
    value_sums = add_rows(lax.all_gather(value_weight, "pts", axis=1, tiled=True))
    valid = jnp.arange(rows) < counts[0, 0]
    key_feats = feature_map(summed_keys).astype(jnp.bfloat16)
    key_feats = jnp.where(valid[:, None], key_feats, jnp.zeros_like(key_feats))
    value_rows = value_sums.astype(jnp.bfloat16)
    local_state = jnp.einsum(
        "yzl,yzn->zln",
        key_feats.reshape(rows, heads, HEAD_DIM),
        value_rows.reshape(rows, heads, HEAD_DIM),
        preferred_element_type=jnp.float32,
    ).reshape(width, HEAD_DIM)
    local_total = jnp.sum(key_feats.astype(jnp.float32), axis=0)
    part_state, part_total = (
        lax.all_gather(local_state[None], "sec", axis=0, tiled=True),
        lax.all_gather(local_total[None], "sec", axis=0, tiled=True),
    )
    state_matrices, totals = lax.psum((part_state, part_total), "pts")
    query_feats = feature_map(
        jnp.dot(normed, query_weight, preferred_element_type=jnp.float32)
    ).astype(jnp.bfloat16)
    query_feats = lax.optimization_barrier(query_feats)
    per_head_queries = query_feats.astype(jnp.float32).reshape(rows, heads, HEAD_DIM)
    state_heads = state_matrices.reshape(sections, heads, HEAD_DIM, HEAD_DIM)
    total_heads = totals.reshape(sections, heads, HEAD_DIM)
    numerator = jnp.einsum(
        "rhk,shkv->srhv", per_head_queries, state_heads, precision=lax.Precision.HIGHEST
    )
    denom = jnp.einsum(
        "rhk,shk->srh", per_head_queries, total_heads, precision=lax.Precision.HIGHEST
    )
    attended = (
        jnp.sum(numerator / denom[:, :, :, None], axis=0).reshape(rows, width).astype(jnp.bfloat16)
    )
    mixed = block.astype(jnp.float32) + jnp.dot(
        attended, output_weight, preferred_element_type=jnp.float32
    )
    centred = layer_normalizer(mixed, middle_gain).astype(jnp.bfloat16)
    shared = broadcast(centred, "sec", sections - 1)
    hidden = jax.nn.gelu(
        jnp.dot(shared, up_weight, preferred_element_type=jnp.float32), approximate=True
    ).astype(jnp.bfloat16)
    is_query = (lax.axis_index("sec") == sections - 1).astype(jnp.float32)
    term = jnp.dot(hidden, down_weight, preferred_element_type=jnp.float32) + is_query * mixed
    return lax.psum_scatter(term, "sec", scatter_dimension=1, tiled=True).astype(jnp.bfloat16)


def solution(mesh):
    placed = (
        P("sec", "pts", None),
        P("sec", "pts"),
        P("sec", None),
        P("sec", "pts", None),
        P("sec", "pts", None),
        P(),
        P(),
        P(),
        P(None, "sec"),
        P("sec", None),
    )
    return jax.shard_map(
        on_device, mesh=mesh, in_specs=placed, out_specs=P("pts", "sec"), check_vma=False
    )
```

profile of v0, /device:TPU:0, one launch (start us, length us, event | category | flops | bytes accessed | tf_op | source)
XLA Modules:
  0.0 379.7 jit_solution(6094853820137793289)
XLA Ops:
  6.5 0.7 all-gather.7.cloned.1.call-update
  7.3 0.7 all-gather.5.cloned.1.call-update
  8.0 0.0 all-gather.9.cloned.1.call-start
  8.7 4.0 %copy.41 = bf16[1,1024,1024]{1,2,0:T(8,128)(2,1)} copy(bf16[1,1024,1024]{2,1,0:T(8,128)(2,1)} %param.10) | data formatting | bytes 4194304 | tf_op args[0]
  12.7 2.1 convert_reduce_fusion
  14.8 0.1 copy-done.1
  14.9 0.6 fusion.5
  15.5 46.0 %all-gather.7.cloned.1.call-done = bf16[1,1024,1024]{2,1,0:T(8,128)(2,1)} async-done(((bf16[1,128,1024]{2,1,0:T(8,128)(2,1)}), bf16[1,1024,1024]{2,1,0:T(8,128)(2,1)}) %all-gather.7.cloned.1.call-update) | async-done | bytes 2097168 | tf_op jit(solution)/shard_map/all_gather | solution.py:48
  61.5 6.2 %fusion.45 = bf16[1024,1024]{0,1:T(8,128)(2,1)} fusion(bf16[1,1024,1024]{2,1,0:T(8,128)(2,1)} %all-gather.7.cloned.1.call-done, bf16[1,1024,1024]{1,2,0:T(8,128)(2,1)} %copy.41, f32[1024]{0:T(1024)S(1)} %bitcast.76, f32[1024]{0:T(1024)S(1)} %add_rsqrt_fusion.1, f32[1024]{0:T(1024)S(1)} %broadcast_multiply_fusion.1), kind=kOutput, calls=%fused_computation.54 | convolution fusion | flops 2153775104 | bytes 6303744 | tf_op jit(solution)/shard_map/dot_general | solution.py:45
  67.7 43.7 %all-gather.5.cloned.1.call-done = bf16[1,1024,1024]{2,1,0:T(8,128)(2,1)} async-done(((bf16[1,128,1024]{2,1,0:T(8,128)(2,1)}), bf16[1,1024,1024]{2,1,0:T(8,128)(2,1)}) %all-gather.5.cloned.1.call-update) | async-done | bytes 2097168 | tf_op jit(solution)/shard_map/all_gather | solution.py:47
  111.4 6.8 %convert_reduce_fusion.1 = (f32[1024]{0:T(1024)S(1)}, bf16[1024,1024]{0,1:T(8,128)(2,1)S(1)}) fusion(bf16[1,1024,1024]{2,1,0:T(8,128)(2,1)} %all-gather.5.cloned.1.call-done, bf16[1,1024,1024]{1,2,0:T(8,128)(2,1)} %copy.41, f32[1024]{0:T(1024)S(1)} %bitcast.77, f32[1024]{0:T(1024)S(1)} %add_rsqrt_fusion.1, f32[1024]{0:T(1024)S(1)} %broadcast_multiply_fusion.1, ...), kind=kOutput, calls=%fused_computation.37 | convolution fusion | flops 2161114112 | bytes 6308864 | tf_op jit(solution)/shard_map/dot_general | solution.py:45
  118.2 1.5 fusion.61
  119.8 0.0 all-reduce.3.cloned.1.call-start
  119.8 21.2 %all-gather.9.cloned.1.call-done = f32[4,1024,128]{2,1,0:T(8,128)} async-done(((f32[1,1024,128]{2,1,0:T(8,128)}), f32[4,1024,128]{2,1,0:T(8,128)}) %all-gather.9.cloned.1.call-update) | async-done | bytes 2097168 | tf_op jit(solution)/shard_map/all_gather | solution.py:61
  141.0 2.9 copy.43
  143.9 0.2 all-reduce.5.cloned.1.call-start
  144.1 7.6 %fusion.24 = bf16[1024,1024]{0,1:T(8,128)(2,1)} fusion(bf16[1024,1024]{1,0:T(8,128)(2,1)} %param.15, bf16[1,1024,1024]{1,2,0:T(8,128)(2,1)} %copy.41, f32[1024]{0:T(1024)S(1)} %bitcast.78, f32[1024]{0:T(1024)S(1)} %add_rsqrt_fusion.1, f32[1024]{0:T(1024)S(1)} %broadcast_multiply_fusion.1), kind=kOutput, calls=%fused_computation.33 | convolution fusion | flops 2157969408 | bytes 6303744 | tf_op jit(solution)/shard_map/dot_general | solution.py:66
  151.7 5.2 %all-gather = f32[4096]{0:T(1024)S(1)} all-gather(f32[1024]{0:T(1024)S(1)} %get-tuple-element.5), channel_id=2, replica_groups=mesh['sec'=4,'pts'=8] {'sec'}, dimensions={0}, use_global_device_ids=true | all-gather | bytes 20480 | tf_op jit(solution)/shard_map/all_gather | solution.py:62
  156.9 38.3 %psum.22 = f32[4,8,128]{2,0,1:T(4,128)S(1)} all-reduce(f32[4,8,128]{2,0,1:T(4,128)S(1)} %copy.48), channel_id=1, replica_groups=mesh['sec'=4,'pts'=8] {'pts'}, use_global_device_ids=true, to_apply=%region_4.5 | all-reduce | flops 4096 | bytes 32768 | tf_op jit(solution)/shard_map/psum | solution.py:64
  195.2 2.5 convolution_bitcast_fusion
  197.7 49.0 %all-reduce.3.cloned.1.call-done = f32[4,8,128,128]{2,3,0,1:T(8,128)} async-done(((f32[4,8,128,128]{2,3,0,1:T(8,128)}), f32[4,8,128,128]{2,3,0,1:T(8,128)}) %all-reduce.3.cloned.1.call-update) | async-done | bytes 2097168 | tf_op jit(solution)/shard_map/psum | solution.py:64
  246.7 9.9 %fusion = bf16[1024,8,128]{0,2,1:T(8,128)(2,1)S(1)} fusion(f32[4,8,128,128]{2,3,0,1:T(8,128)} %all-reduce.3.cloned.1.call-done, bf16[1024,8,128,1]{0,2,3,1:T(8,128)(2,1)} %bitcast.71, f32[4,1024,8]{1,0,2:T(4,128)S(1)} %convolution_bitcast_fusion), kind=kOutput, calls=%fused_computation.1 | convolution fusion | flops 6449790976 | bytes 6422528 | tf_op jit(solution)/shard_map/rhk,shkv->srhv/dot_general | solution.py:72
  256.7 2.6 fusion.58
  259.4 0.5 multiply_reduce_fusion
  259.9 1.4 copy-done.3
  261.3 2.0 fusion.25
  263.3 0.3 reduce-scatter.2.cloned.1.call-start
  263.5 51.0 %all-reduce.5.cloned.1.call-done = bf16[1024,1024]{0,1:T(8,128)(2,1)} async-done(((bf16[1024,1024]{0,1:T(8,128)(2,1)}), bf16[1024,1024]{0,1:T(8,128)(2,1)}) %all-reduce.5.cloned.1.call-update) | async-done | bytes 2097168 | tf_op jit(solution)/shard_map/psum | solution.py:11
  314.5 11.3 %multiply_add_fusion = f32[1024,1024]{0,1:T(8,128)} fusion(f32[1024,1024]{0,1:T(8,128)} %copy-done.3, f32[]{:T(128)S(6)} %convert_element_type.62, bf16[1024,1024]{1,0:T(8,128)(2,1)} %param.19, bf16[1024,1024]{0,1:T(8,128)(2,1)} %all-reduce.5.cloned.1.call-done, bf16[1024,1024]{1,0:T(8,128)(2,1)} %param.18), kind=kOutput, calls=%fused_computation.34 | convolution fusion | flops 4306501632 | bytes 14680068 | tf_op jit(solution)/shard_map/dot_general | solution.py:90
  325.9 44.7 %reduce-scatter.2.cloned.1.call-done = f32[1024,256]{0,1:T(8,128)} async-done(((f32[1024,1024]{0,1:T(8,128)}), f32[1024,256]{0,1:T(8,128)}) %reduce-scatter.2.cloned.1.call-update) | async-done | bytes 1048592 | tf_op jit(solution)/shard_map/reduce_scatter | solution.py:91
  370.6 1.3 convert_element_type.63
  371.9 1.0 copy.56
  (24 shorter events, 0.2 us)
Async XLA Ops:
  6.5 250.2 %copy-start = (bf16[1024,1024]{1,0:T(8,128)(2,1)S(1)}, bf16[1024,1024]{1,0:T(8,128)(2,1)}, u32[]{:S(2)}) copy-start(bf16[1024,1024]{1,0:T(8,128)(2,1)} %param.16) | copy-start | bytes 6291460
  6.5 55.0 %all-gather.7.cloned.1.call-start = ((), (), s32[]{:S(2)}) async-start(), calls=%async_computation.2 | async-start | bytes 2359296 | tf_op jit(solution)/shard_map/all_gather | solution.py:48
  7.3 104.2 %all-gather.5.cloned.1.call-start = ((), (), s32[]{:S(2)}) async-start(), calls=%async_computation.1 | async-start | bytes 2359296 | tf_op jit(solution)/shard_map/all_gather | solution.py:47
  8.0 133.0 %all-gather.9.cloned.1.call-start = ((), (), s32[]{:S(2)}) async-start(), calls=%async_computation.3 | async-start | bytes 2621440 | tf_op jit(solution)/shard_map/all_gather | solution.py:61
  12.7 2.2 copy-start.1
  12.7 48.8 %copy-start.6 = (f32[1,1024]{1,0:T(1,128)S(1)}, f32[1,1024]{1,0:T(1,128)}, u32[]{:S(2)}) copy-start(f32[1,1024]{1,0:T(1,128)} %param.12) | copy-start | bytes 12292
  111.4 6.8 %copy-start.4 = (bf16[1024,1024]{0,1:T(8,128)(2,1)S(1)}, bf16[1024,1024]{0,1:T(8,128)(2,1)}, u32[]{:S(2)}) copy-start(bf16[1024,1024]{0,1:T(8,128)(2,1)} %fusion.45) | copy-start | bytes 6291460
  119.8 127.0 %all-reduce.3.cloned.1.call-start = ((), (), s32[]{:S(2)}) async-start(), calls=%async_computation.4 | async-start | bytes 4194304 | tf_op jit(solution)/shard_map/psum | solution.py:64
  143.9 170.6 %all-reduce.5.cloned.1.call-start = ((), (), s32[]{:S(2)}) async-start(), calls=%async_computation.5 | async-start | bytes 4194304 | tf_op jit(solution)/shard_map/psum | solution.py:11
  246.7 10.0 %copy-start.2 = (bf16[1,1024,1024]{1,2,0:T(8,128)(2,1)S(1)}, bf16[1,1024,1024]{1,2,0:T(8,128)(2,1)}, u32[]{:S(2)}) copy-start(bf16[1,1024,1024]{1,2,0:T(8,128)(2,1)} %copy.41) | copy-start | bytes 6291460
  259.3 1.9 copy-start.3
  259.4 1.9 copy-start.5
  263.3 107.3 %reduce-scatter.2.cloned.1.call-start = ((), (), s32[]{:S(2)}) async-start(), calls=%async_computation.6 | async-start | bytes 5242880 | tf_op jit(solution)/shard_map/reduce_scatter | solution.py:91
Sparse Core Ops, SparseCore 0:
  9.5 51.9 all-gather.6
  63.6 47.7 all-gather.4
  119.9 21.0 all-gather.8
  144.5 102.2 all-reduce.2
  263.4 51.1 all-reduce.4
  326.0 44.5 reduce-scatter.1
where the time goes:
time: 380 us
  waiting for transfers between devices  257 us (68%)
  matrix products  48.4 us (13%)
  blocking collectives  43.5 us (11%)
  between operations  14.2 us (4%)
  local copies, waits for them, and re-layouts  9.38 us (2%)
  other arithmetic  6.49 us (2%)
    psum x1, waiting for transfers between devices, broadcast(): return lax.psum(jnp.where(mine, value, jnp.zeros_like(value)), axis)  51 us
    psum x1, waiting for transfers between devices, on_device(): state_matrices, totals = lax.psum((part_state, part_total), 'pts')  49 us
    all_gather x1, waiting for transfers between devices, on_device(): lax.all_gather(value_weight, 'pts', axis=1, tiled=True)  46 us
    reduce_scatter x1, waiting for transfers between devices, on_device(): lax.psum_scatter(term, 'sec', scatter_dimension=1, tiled=True)  44.7 us
    all_gather x1, waiting for transfers between devices, on_device(): lax.all_gather(key_weight, 'pts', axis=1, tiled=True)  43.7 us
    psum x1, blocking collectives, on_device(): state_matrices, totals = lax.psum((part_state, part_total), 'pts')  38.3 us
    all_gather x1, waiting for transfers between devices, on_device(): lax.all_gather(local_state[None], 'sec', axis=0, tiled=True)  21.2 us
    dot_general x2, matrix products, add_rows(): return jnp.dot(normed, piece[0], preferred_element_type=jnp.float32)  13 us
  transfers between devices with their start and end apart: 6, of which 6 were waited for; matrix products, arithmetic and copies ran while one was open for 6% of the time, Pallas kernels for 0%

commit v1 on v0

v1 whole, which is shorter than its diff:
```python
import functools

import jax
import jax.numpy as jnp
from jax import lax
from jax.experimental import pallas as pl
from jax.experimental.pallas import tpu as pltpu
from jax.sharding import PartitionSpec as P

HEAD_DIM = 128
EXTRA = 16
MESH = pl.DeviceIdType.MESH
DMA = pltpu.SemaphoreType.DMA
VMEM_LIMIT = 48 * 1024 * 1024


def layer_normalizer(values, gain):
    mean = jnp.mean(values, axis=-1, keepdims=True)
    centred = values - mean
    spread = jnp.mean(centred * centred, axis=-1, keepdims=True)
    return centred * lax.rsqrt(spread + 1e-05) * gain


def feature_map(values):
    return jax.nn.elu(values) + 1.0


def sibling_of(sec):
    return sec + 1 - 2 * lax.rem(sec, 2)


def across_of(sec):
    return lax.rem(sec + 2, 4)


def remote(src, dst, send_sem, recv_sem, **where):
    return pltpu.make_async_remote_copy(
        src_ref=src,
        dst_ref=dst,
        send_sem=send_sem,
        recv_sem=recv_sem,
        device_id=where,
        device_id_type=MESH,
    )


def gather_kernel(
    blocks, sections, key_ref, value_ref, points_ref, gain_ref,
    wk_ref, wv_ref, query_ref, query_gain_ref,
    local_sem, up_sem, down_sem, pair_sem, line_recv, pair_recv, query_send, query_recv, gain_send, gain_recv,
):
    length = blocks // 2
    depth = key_ref.shape[0]
    share = query_ref.shape[0]
    sec = lax.axis_index("sec")
    me = lax.axis_index("pts")
    spot, side = me // 2, lax.rem(me, 2)
    pair = spot * 2 + 1 - side
    owner = sections - 1
    barrier = pltpu.get_barrier_semaphore()
    for other in (lax.rem(spot + 1, length) * 2 + side, lax.rem(spot + length - 1, length) * 2 + side, pair):
        pl.semaphore_signal(barrier, inc=1, device_id={"pts": other}, device_id_type=MESH)
    for step in range(1, sections):
        pl.semaphore_signal(
            barrier, inc=1, device_id={"sec": lax.rem(sec + step, sections)}, device_id_type=MESH
        )
    pl.semaphore_wait(barrier, 3 + sections - 1)

    def query_copy(to):
        return remote(
            points_ref.at[pl.ds(to * share, share)], query_ref, query_send.at[to], query_recv, sec=to
        )

    def gain_copy(to):
        return remote(gain_ref, query_gain_ref, gain_send.at[to], gain_recv, sec=to)

    def kept_query():
        return pltpu.make_async_copy(
            points_ref.at[pl.ds(owner * share, share)], query_ref, local_sem.at[2]
        )

    def kept_gain():
        return pltpu.make_async_copy(gain_ref, query_gain_ref, local_sem.at[3])

    @pl.when(sec == owner)
    def _():
        for to in range(owner):
            gain_copy(to).start()
            query_copy(to).start()
        kept_query().start()
        kept_gain().start()

    shards = (key_ref, value_ref)
    wholes = (wk_ref, wv_ref)

    def place(which, index):
        return wholes[which].at[pl.ds(pl.multiple_of(index * depth, depth), depth)]

    def line_copy(which, source, step, own):
        here = place(which, source * 2 + side)
        sems = up_sem if step > 0 else down_sem
        return remote(
            shards[which] if own else here, here, sems.at[which, source], line_recv.at[which, source],
            pts=(spot + step) * 2 + side,
        )

    def pair_copy(which, source, own):
        here = place(which, source * 2 + side)
        return remote(
            shards[which] if own else here, here, pair_sem.at[which, source], pair_recv.at[which, source],
            pts=pair,
        )

    def kept(which):
        return pltpu.make_async_copy(shards[which], place(which, me), local_sem.at[which])

    for which in range(2):
        @pl.when(spot < length - 1)
        def _():
            line_copy(which, spot, 1, True).start()

        @pl.when(spot > 0)
        def _():
            line_copy(which, spot, -1, True).start()

        pair_copy(which, spot, True).start()
    for which in range(2):
        kept(which).start()
    for distance in range(1, length):
        for which in range(2):
            @pl.when(spot - distance >= 0)
            def _():
                source = spot - distance
                line_copy(which, source, 1, False).wait_recv()

                @pl.when(spot < length - 1)
                def _():
                    line_copy(which, source, 1, False).start()

                pair_copy(which, source, False).start()

            @pl.when(spot + distance < length)
            def _():
                source = spot + distance
                line_copy(which, source, -1, False).wait_recv()

                @pl.when(spot > 0)
                def _():
                    line_copy(which, source, -1, False).start()

                pair_copy(which, source, False).start()

    for source in range(length):
        for which in range(2):
            there = place(which, source * 2 + 1 - side)
            remote(
                there, there, pair_sem.at[which, source], pair_recv.at[which, source], pts=pair
            ).wait_recv()
    for source in range(length):
        for which in range(2):
            pair_copy(which, source, False).wait_send()

            @pl.when(jnp.logical_and(spot < length - 1, source <= spot))
            def _():
                line_copy(which, source, 1, False).wait_send()

            @pl.when(jnp.logical_and(spot > 0, source >= spot))
            def _():
                line_copy(which, source, -1, False).wait_send()

    for which in range(2):
        kept(which).wait()

    @pl.when(sec == owner)
    def _():
        for to in range(owner):
            gain_copy(to).wait_send()
            query_copy(to).wait_send()
        kept_query().wait()
        kept_gain().wait()

    @pl.when(sec != owner)
    def _():
        gain_copy(0).wait_recv()
        query_copy(0).wait_recv()


def gather_projections(blocks, sections, key, value, points, gain):
    depth, width = key.shape
    rows = points.shape[0]
    length = blocks // 2
    anywhere = pl.BlockSpec(memory_space=pl.ANY)
    return pl.pallas_call(
        functools.partial(gather_kernel, blocks, sections),
        out_shape=(
            jax.ShapeDtypeStruct((depth * blocks, width), key.dtype),
            jax.ShapeDtypeStruct((depth * blocks, width), value.dtype),
            jax.ShapeDtypeStruct((rows // sections, width), points.dtype),
            jax.ShapeDtypeStruct(gain.shape, gain.dtype),
        ),
        in_specs=[anywhere] * 4,
        out_specs=(anywhere,) * 4,
        scratch_shapes=[
            DMA((4,)),
            DMA((2, length)),
            DMA((2, length)),
            DMA((2, length)),
            DMA((2, length)),
            DMA((2, length)),
            DMA((sections,)),
            DMA,
            DMA((sections,)),
            DMA,
        ],
        compiler_params=pltpu.CompilerParams(
            collective_id=0, has_side_effects=True, vmem_limit_bytes=VMEM_LIMIT
        ),
    )(key, value, points, gain)


def state_kernel(
    blocks, part_ref, out_ref, landed, part_send, part_recv, share_send, share_recv, across_send, across_recv,
    near_send, near_recv,
):
    sec = lax.axis_index("sec")
    me = lax.axis_index("pts")
    near, across = sibling_of(sec), across_of(sec)
    barrier = pltpu.get_barrier_semaphore()
    for step in range(1, blocks):
        pl.semaphore_signal(
            barrier, inc=1, device_id={"pts": lax.rem(me + step, blocks)}, device_id_type=MESH
        )
    for other in (near, across):
        pl.semaphore_signal(barrier, inc=1, device_id={"sec": other}, device_id_type=MESH)
    pl.semaphore_wait(barrier, blocks + 1)

    def part_copy(step):
        to = lax.rem(me + step, blocks)
        return remote(part_ref.at[to], landed.at[step], part_send.at[step], part_recv.at[step], pts=to)

    def share_copy(step):
        mine = out_ref.at[sec, me]
        return remote(mine, mine, share_send.at[step], share_recv.at[step], pts=lax.rem(me + step, blocks))

    def arriving(step):
        slot = out_ref.at[sec, lax.rem(me + blocks - step, blocks)]
        return remote(slot, slot, share_send.at[step], share_recv.at[step], pts=me)

    def across_copy(step):
        slot = out_ref.at[sec, lax.rem(me + blocks - step, blocks)]
        return remote(slot, slot, across_send.at[step], across_recv.at[step], sec=across)

    def across_arriving(step):
        slot = out_ref.at[across, lax.rem(me + blocks - step, blocks)]
        return remote(slot, slot, across_send.at[step], across_recv.at[step], sec=across)

    def near_copy(kind, step):
        slot = out_ref.at[across if kind else sec, lax.rem(me + blocks - step, blocks)]
        return remote(slot, slot, near_send.at[kind, step], near_recv.at[kind, step], sec=near)

    def near_arriving(kind, step):
        slot = out_ref.at[across_of(near) if kind else near, lax.rem(me + blocks - step, blocks)]
        return remote(slot, slot, near_send.at[kind, step], near_recv.at[kind, step], sec=near)

    for step in range(1, blocks):
        part_copy(step).start()
    total = part_ref[me].astype(jnp.float32)
    for step in range(1, blocks):
        part_copy(step).wait_recv()
        total += landed[step].astype(jnp.float32)
    out_ref[sec, me] = total.astype(out_ref.dtype)
    for step in range(1, blocks):
        share_copy(step).start()
    for step in range(blocks):
        if step:
            arriving(step).wait_recv()
        across_copy(step).start()
        near_copy(0, step).start()
    for step in range(blocks):
        across_arriving(step).wait_recv()
        near_copy(1, step).start()
    for step in range(blocks):
        near_arriving(0, step).wait_recv()
        near_arriving(1, step).wait_recv()
    for step in range(1, blocks):
        part_copy(step).wait_send()
        share_copy(step).wait_send()
    for step in range(blocks):
        across_copy(step).wait_send()
        near_copy(0, step).wait_send()
        near_copy(1, step).wait_send()


def sum_states(blocks, sections, parts):
    inside = pl.BlockSpec(memory_space=pltpu.VMEM)
    return pl.pallas_call(
        functools.partial(state_kernel, blocks),
        out_shape=jax.ShapeDtypeStruct((sections,) + parts.shape, parts.dtype),
        in_specs=[inside],
        out_specs=inside,
        scratch_shapes=[
            pltpu.VMEM(parts.shape, parts.dtype),
            DMA((blocks,)),
            DMA((blocks,)),
            DMA((blocks,)),
            DMA((blocks,)),
            DMA((blocks,)),
            DMA((blocks,)),
            DMA((2, blocks)),
            DMA((2, blocks)),
        ],
        compiler_params=pltpu.CompilerParams(
            collective_id=1, has_side_effects=True, vmem_limit_bytes=VMEM_LIMIT
        ),
    )(parts)


def feed_kernel(
    centred_ref, mixed_ref, up_ref, down_ref, out_ref,
    rows_in, sums, own, cross, to_near, from_near, to_across, from_across,
    gather_send, gather_recv, near_send, near_recv, across_send, across_recv,
):
    sec = lax.axis_index("sec")
    near, across = sibling_of(sec), across_of(sec)
    corner = sibling_of(across)
    share = centred_ref.shape[0]
    columns = out_ref.shape[1]
    barrier = pltpu.get_barrier_semaphore()
    for other in (near, across):
        pl.semaphore_signal(barrier, inc=1, device_id={"sec": other}, device_id_type=MESH)
    pl.semaphore_wait(barrier, 2)

    to_x = remote(centred_ref, rows_in.at[sec], gather_send.at[0], gather_recv.at[sec], sec=across)
    to_n = remote(centred_ref, rows_in.at[sec], gather_send.at[1], gather_recv.at[sec], sec=near)
    pass_on = remote(rows_in.at[across], rows_in.at[across], gather_send.at[2], gather_recv.at[across], sec=near)

    def landing(block):
        return remote(rows_in.at[block], rows_in.at[block], gather_send.at[2], gather_recv.at[block], sec=near)

    def near_copy(block):
        return remote(to_near.at[block], from_near.at[block], near_send.at[block], near_recv.at[block], sec=near)

    def across_copy(block):
        return remote(
            to_across.at[block], from_across.at[block], across_send.at[block], across_recv.at[block], sec=across
        )

    to_x.start()
    to_n.start()
    span = 256
    steps = up_ref.shape[1] // span

    def run(source, first):
        if first:
            sums[...] = mixed_ref[...]
        else:
            sums[...] = jnp.zeros_like(sums)

        @pl.loop(0, steps)
        def _(step):
            units = pl.ds(pl.multiple_of(step * span, span), span)
            hidden = jax.nn.gelu(
                jnp.dot(source[...], up_ref[:, units], preferred_element_type=jnp.float32), approximate=True
            ).astype(jnp.bfloat16)
            sums[...] += jnp.dot(hidden, down_ref[units, :], preferred_element_type=jnp.float32)

    def part(of):
        return sums[:, pl.ds(pl.multiple_of(of * columns, columns), columns)]

    low = lax.rem(near, 2)

    def emit(block):
        own[block] = part(sec)
        cross[block] = part(across)
        to_near[block, 0] = part(low).astype(jnp.bfloat16)
        to_near[block, 1] = part(low + 2).astype(jnp.bfloat16)
        near_copy(block).start()

    def forward(block):
        near_copy(block).wait_recv()
        to_across[block] = (cross[block] + from_near[block, across // 2].astype(jnp.float32)).astype(jnp.bfloat16)
        across_copy(block).start()

    run(centred_ref, True)
    emit(sec)
    landing(near).wait_recv()
    run(rows_in.at[near], False)
    emit(near)
    forward(near)
    forward(sec)
    landing(across).wait_recv()
    pass_on.start()
    run(rows_in.at[across], False)
    emit(across)
    landing(corner).wait_recv()
    run(rows_in.at[corner], False)
    emit(corner)
    forward(corner)
    forward(across)
    for block in (near, sec, corner, across):
        across_copy(block).wait_recv()
        out_ref[pl.ds(pl.multiple_of(block * share, share), share), :] = (
            own[block] + from_near[block, sec // 2].astype(jnp.float32) + from_across[block].astype(jnp.float32)
        ).astype(out_ref.dtype)
    for block in (near, sec, corner, across):
        near_copy(block).wait_send()
        across_copy(block).wait_send()
    to_x.wait_send()
    to_n.wait_send()
    pass_on.wait_send()


def feed_forward(sections, centred, mixed, up, down):
    share, width = centred.shape
    columns = width // sections
    inside = pl.BlockSpec(memory_space=pltpu.VMEM)
    half = jnp.bfloat16
    return pl.pallas_call(
        feed_kernel,
        out_shape=jax.ShapeDtypeStruct((share * sections, columns), half),
        in_specs=[inside] * 4,
        out_specs=inside,
        scratch_shapes=[
            pltpu.VMEM((sections, share, width), half),
            pltpu.VMEM((share, width), jnp.float32),
            pltpu.VMEM((sections, share, columns), jnp.float32),
            pltpu.VMEM((sections, share, columns), jnp.float32),
            pltpu.VMEM((sections, 2, share, columns), half),
            pltpu.VMEM((sections, 2, share, columns), half),
            pltpu.VMEM((sections, share, columns), half),
            pltpu.VMEM((sections, share, columns), half),
            DMA((3,)),
            DMA((sections,)),
            DMA((sections,)),
            DMA((sections,)),
            DMA((sections,)),
            DMA((sections,)),
        ],
        compiler_params=pltpu.CompilerParams(
            collective_id=2, has_side_effects=True, vmem_limit_bytes=VMEM_LIMIT
        ),
    )(centred, mixed, up, down)


def on_device(
    points,
    counts,
    input_gain,
    key_weight,
    value_weight,
    query_weight,
    output_weight,
    middle_gain,
    up_weight,
    down_weight,
):
    block = points[0]
    rows, width = block.shape
    heads = width // HEAD_DIM
    sections = lax.axis_size("sec")
    blocks = lax.axis_size("pts")
    whole_key, whole_value, query_rows, query_gain = gather_projections(
        blocks, sections, key_weight[0], value_weight[0], block, input_gain.reshape(heads, HEAD_DIM)
    )
    normed = layer_normalizer(block.astype(jnp.float32), input_gain[0]).astype(jnp.bfloat16)
    valid = jnp.arange(rows) < counts[0, 0]
    key_feats = feature_map(
        jnp.dot(normed, whole_key, preferred_element_type=jnp.float32)
    ).astype(jnp.bfloat16)
    key_feats = jnp.where(valid[:, None], key_feats, jnp.zeros_like(key_feats))
    value_rows = jnp.dot(normed, whole_value, preferred_element_type=jnp.float32).astype(jnp.bfloat16)
    local_state = jnp.einsum(
        "yzl,yzn->zln",
        key_feats.reshape(rows, heads, HEAD_DIM),
        value_rows.reshape(rows, heads, HEAD_DIM),
        preferred_element_type=jnp.float32,
    ).reshape(width, HEAD_DIM)
    local_total = jnp.sum(key_feats.astype(jnp.float32), axis=0)
    slab = width // blocks
    extra = jnp.pad(local_total.reshape(blocks, 1, slab), ((0, 0), (0, EXTRA - 1), (0, HEAD_DIM - slab)))
    parts = jnp.concatenate([local_state.reshape(blocks, slab, HEAD_DIM), extra], axis=1).astype(jnp.bfloat16)
    summed = sum_states(blocks, sections, parts)
    state_heads = summed[:, :, :slab].reshape(sections, heads, HEAD_DIM, HEAD_DIM)
    total_heads = summed[:, :, slab, :slab].reshape(sections, heads, HEAD_DIM)

    query_wide = query_rows.astype(jnp.float32)
    query_normed = layer_normalizer(query_wide, query_gain.reshape(width)).astype(jnp.bfloat16)
    query_feats = feature_map(
        jnp.dot(query_normed, query_weight, preferred_element_type=jnp.float32)
    ).astype(jnp.bfloat16)
    share = query_rows.shape[0]
    per_head_queries = query_feats.reshape(share, heads, HEAD_DIM)
    numerator = jnp.einsum(
        "rhk,shkv->srhv", per_head_queries, state_heads, preferred_element_type=jnp.float32
    )
    denom = jnp.einsum("rhk,shk->srh", per_head_queries, total_heads, preferred_element_type=jnp.float32)
    attended = (
        jnp.sum(numerator / denom[:, :, :, None], axis=0).reshape(share, width).astype(jnp.bfloat16)
    )
    mixed = query_wide + jnp.dot(attended, output_weight, preferred_element_type=jnp.float32)
    centred = layer_normalizer(mixed, middle_gain).astype(jnp.bfloat16)
    return feed_forward(sections, centred, mixed, up_weight, down_weight)


def solution(mesh):
    placed = (
        P("sec", "pts", None),
        P("sec", "pts"),
        P("sec", None),
        P("sec", "pts", None),
        P("sec", "pts", None),
        P(),
        P(),
        P(),
        P(None, "sec"),
        P("sec", None),
    )
    return jax.shard_map(
        on_device, mesh=mesh, in_specs=placed, out_specs=P("pts", "sec"), check_vma=False
    )
```

time: 380 us -> 124 us (0.33)
  waiting for transfers between devices: 257 us -> 0 us
  Pallas kernels: 0 us -> 105 us
  blocking collectives: 43.5 us -> 0 us
  matrix products: 48.4 us -> 11.6 us
  between operations: 14.2 us -> 0.85 us
  local copies, waits for them, and re-layouts: 9.38 us -> 4.79 us
  other arithmetic: 6.49 us -> 2 us
    all_gather x3 -> x0, waiting for transfers between devices: 111 us -> none  [the longest x1 46 us: on_device(): lax.all_gather(value_weight, 'pts', axis=1, tiled=True)]
    pallas_call x0 -> x3, Pallas kernels: none -> 105 us  [the longest x1 52.4 us: gather_projections(): pl.pallas_call(functools.partial(gather_kernel, blocks, sections), out_sh...]
    psum x2 -> x0, waiting for transfers between devices: 100 us -> none  [the longest x1 51 us: broadcast(): return lax.psum(jnp.where(mine, value, jnp.zeros_like(value)), axis)]
    reduce_scatter x1 -> x0, waiting for transfers between devices: 44.7 us -> none  [on_device(): lax.psum_scatter(term, 'sec', scatter_dimension=1, tiled=True)]
    psum x1 -> x0, blocking collectives: 38.3 us -> none  [on_device(): state_matrices, totals = lax.psum((part_state, part_total), 'pts')]
    dot_general x6 -> x5, matrix products: 44.3 us -> 9.91 us  [the longest x1 4.98 us: on_device(): jnp.dot(normed, whole_key, preferred_element_type=jnp.float32)]
    all_gather x1 -> x0, blocking collectives: 5.17 us -> none  [on_device(): lax.all_gather(local_total[None], 'sec', axis=0, tiled=True)]
  transfers between devices with their start and end apart: 6 -> 0, of which waited for: 6 -> 0; matrix products, arithmetic and copies ran while one was open for 6% -> 0% of each run, Pallas kernels for 0% -> 0%
where the time goes in v1:
time: 124 us
  Pallas kernels  105 us (85%)
  matrix products  11.6 us (9%)
  local copies, waits for them, and re-layouts  4.79 us (4%)
  other arithmetic  2 us (2%)
    pallas_call x1, Pallas kernels, gather_projections(): pl.pallas_call(functools.partial(gather_kernel, blocks, sections), out_sh...  52.4 us
    pallas_call x1, Pallas kernels, feed_forward(): pl.pallas_call(feed_kernel, out_shape=jax.ShapeDtypeStruct((share * secti...  29.4 us
    pallas_call x1, Pallas kernels, sum_states(): pl.pallas_call(functools.partial(state_kernel, blocks), out_shape=jax.Sha...  23.1 us
    dot_general x1, matrix products, on_device(): jnp.dot(normed, whole_key, preferred_element_type=jnp.float32)  4.98 us
    unnamed x18, local copies, waits for them, and re-layouts  4.77 us
    dot_general x1, matrix products, on_device(): jnp.dot(normed, whole_value, preferred_element_type=jnp.float32)  2.81 us

profile of v1, /device:TPU:0, one launch (start us, length us, event | category | flops | bytes accessed | tf_op | source)
XLA Modules:
  0.0 124.1 jit_solution(4236710162575549350)
XLA Ops:
  0.0 0.0 copy-start
  0.0 0.0 copy-start.2
  0.0 1.1 copy-done.2
  1.1 0.0 copy-start.3
  1.1 0.9 copy-done.3
  2.1 0.0 copy-start.4
  2.1 0.7 copy-done.4
  2.7 52.4 %shard_map.100 = (bf16[1024,1024]{1,0:T(8,128)(2,1)S(1)}, bf16[1024,1024]{1,0:T(8,128)(2,1)S(1)}, bf16[256,1024]{1,0:T(8,128)(2,1)S(1)}, f32[8,128]{1,0:T(8,128)S(1)}) custom-call(bf16[128,1024]{1,0:T(8,128)(2,1)S(1)} %bitcast.48, bf16[128,1024]{1,0:T(8,128)(2,1)S(1)} %bitcast.49, bf16[1024,1024]{1,0:T(8,128)(2,1)} %bitcast.54, f32[8,128]{1,0:T(8,128)S(1)} %bitcast.50), custom_call_target="tpu_custom_call" | custom-call | tf_op jit(solution)/shard_map/pallas_call | solution.py:193
  55.2 0.0 copy-done.5
  55.2 0.3 convert_reduce_fusion
  55.5 0.7 fusion.2
  56.9 5.0 %fusion.38 = (bf16[1024]{0:T(1024)(128)(2,1)S(1)}, bf16[1024,1024]{0,1:T(8,128)(2,1)S(1)}) fusion(bf16[1024,1024]{1,0:T(8,128)(2,1)S(1)} %get-tuple-element.10, f32[1024]{0:T(1024)S(1)} %bitcast.51, f32[1024]{0:T(1024)S(1)} %add_rsqrt_fusion, f32[1024]{0:T(1024)S(1)} %broadcast_multiply_fusion, bf16[1,1024,1024]{2,1,0:T(8,128)(2,1)S(1)} %copy-done.5, ...), kind=kOutput, calls=%fused_computation.54 | convolution fusion | flops 2160065536 | bytes 6306816 | tf_op jit(solution)/shard_map/dot_general | solution.py:468
  61.9 2.8 %convolution_convert_fusion = bf16[1024,1024]{0,1:T(8,128)(2,1)S(1)} fusion(bf16[1024,1024]{1,0:T(8,128)(2,1)S(1)} %get-tuple-element.11, f32[1024]{0:T(1024)S(1)} %bitcast.52, f32[1024]{0:T(1024)S(1)} %add_rsqrt_fusion, f32[1024]{0:T(1024)S(1)} %broadcast_multiply_fusion, bf16[1,1024,1024]{2,1,0:T(8,128)(2,1)S(1)} %copy-done.5), kind=kOutput, calls=%fused_computation.17 | convolution fusion | flops 2153775104 | bytes 6303744 | tf_op jit(solution)/shard_map/dot_general | solution.py:471
  64.7 0.9 convolution_convert_fusion.1
  65.6 0.0 copy-start.7
  65.7 23.1 %shard_map.101 = bf16[4,8,144,128]{3,2,1,0:T(8,128)(2,1)S(1)} custom-call(bf16[8,144,128]{2,1,0:T(8,128)(2,1)S(1)} %fusion.30.part_ref), custom_call_target="tpu_custom_call" | custom-call | tf_op jit(solution)/shard_map/pallas_call | solution.py:296
  88.8 0.1 convert_reduce_fusion.1
  88.9 0.3 fusion.12
  89.2 0.0 copy-done.7
  89.3 1.1 fusion.17
  90.4 0.2 convolution_bitcast_fusion
  90.6 0.1 copy.36
  90.7 0.8 fusion.8
  91.5 0.0 copy-done
  91.5 0.0 copy-start.6
  91.5 0.8 fusion.39
  92.4 0.2 multiply_reduce_fusion
  92.7 0.0 copy-done.6
  92.7 0.2 multiply_convert_fusion.centred_ref
  92.9 1.1 copy-done.1
  94.0 29.4 %shard_map.102 = bf16[1024,256]{1,0:T(8,128)(2,1)S(1)} custom-call(bf16[256,1024]{1,0:T(8,128)(2,1)S(1)} %multiply_convert_fusion.centred_ref, f32[256,1024]{1,0:T(8,128)S(1)} %get-tuple-element.16.mixed_ref, bf16[1024,1024]{1,0:T(8,128)(2,1)S(1)} %copy-done.1, bf16[1024,1024]{1,0:T(8,128)(2,1)} %down_ref.1), custom_call_target="tpu_custom_call" | custom-call | tf_op jit(solution)/shard_map/pallas_call | solution.py:418
  123.3 0.8 copy.51
  (12 shorter events, 0.1 us)
Async XLA Ops:
  0.0 91.5 %copy-start = (bf16[1024,1024]{1,0:T(8,128)(2,1)S(1)}, bf16[1024,1024]{1,0:T(8,128)(2,1)}, u32[]{:S(2)}) copy-start(bf16[1024,1024]{1,0:T(8,128)(2,1)} %param.16) | copy-start | bytes 6291460
  0.0 1.1 copy-start.2
  1.1 0.9 copy-start.3
  2.1 0.7 copy-start.4
  2.7 52.4 %copy-start.5 = (bf16[1,1024,1024]{2,1,0:T(8,128)(2,1)S(1)}, bf16[1,1024,1024]{2,1,0:T(8,128)(2,1)}, u32[]{:S(2)}) copy-start(bf16[1,1024,1024]{2,1,0:T(8,128)(2,1)} %param.10) | copy-start | bytes 6291460
  65.6 23.6 %copy-start.7 = (bf16[1024,1024]{1,0:T(8,128)(2,1)S(1)}, bf16[1024,1024]{1,0:T(8,128)(2,1)}, u32[]{:S(2)}) copy-start(bf16[1024,1024]{1,0:T(8,128)(2,1)} %param.15) | copy-start | bytes 6291460
  91.5 1.1 copy-start.6
  92.4 1.6 %copy-start.1 = (bf16[1024,1024]{1,0:T(8,128)(2,1)S(1)}, bf16[1024,1024]{1,0:T(8,128)(2,1)}, u32[]{:S(2)}) copy-start(bf16[1024,1024]{1,0:T(8,128)(2,1)} %up_ref.1) | copy-start | bytes 6291460

commit v2 on v1

v2 whole, which is shorter than its diff:
```python
import functools

import jax
import jax.numpy as jnp
from jax import lax
from jax.experimental import pallas as pl
from jax.experimental.pallas import tpu as pltpu
from jax.sharding import PartitionSpec as P

HEAD_DIM = 128
EXTRA = 16
MESH = pl.DeviceIdType.MESH
DMA = pltpu.SemaphoreType.DMA
VMEM_LIMIT = 48 * 1024 * 1024


def layer_normalizer(values, gain):
    mean = jnp.mean(values, axis=-1, keepdims=True)
    centred = values - mean
    spread = jnp.mean(centred * centred, axis=-1, keepdims=True)
    return centred * lax.rsqrt(spread + 1e-05) * gain


def feature_map(values):
    return jax.nn.elu(values) + 1.0


def sibling_of(sec):
    return sec + 1 - 2 * lax.rem(sec, 2)


def across_of(sec):
    return lax.rem(sec + 2, 4)


def remote(src, dst, send_sem, recv_sem, **where):
    return pltpu.make_async_remote_copy(
        src_ref=src,
        dst_ref=dst,
        send_sem=send_sem,
        recv_sem=recv_sem,
        device_id=where,
        device_id_type=MESH,
    )


def gather_kernel(
    blocks, sections, shard_ref, points_ref, aux_ref,
    whole_ref, rows_ref, rows_aux_ref, query_ref, query_aux_ref,
    local_sem, up_sem, down_sem, near_sem, pair_sem, recv_sem, swap_send, swap_recv, query_send, query_recv,
):
    length = blocks // 2
    depth = shard_ref.shape[1]
    share = query_ref.shape[0]
    sec = lax.axis_index("sec")
    me = lax.axis_index("pts")
    spot, side = me // 2, lax.rem(me, 2)
    core = lax.rem(sec, 2)
    base = sec - core
    near = base + 1 - core
    pair = spot * 2 + 1 - side
    owner = sections - 1
    barrier = pltpu.get_barrier_semaphore()

    def greet(**where):
        pl.semaphore_signal(barrier, inc=1, device_id=where, device_id_type=MESH)

    for other in (near, across_of(sec), across_of(near)):
        greet(sec=other)
    for step in (1, length - 1):
        beside = lax.rem(spot + step, length) * 2 + side
        greet(pts=beside)
        greet(sec=near, pts=beside)
    greet(pts=pair)
    greet(sec=near, pts=pair)
    pl.semaphore_wait(barrier, 9)

    def place(which, index):
        return whole_ref.at[which, pl.ds(pl.multiple_of(index * depth, depth), depth)]

    def copy(which, index, sem, own, **where):
        here = place(which, index)
        return remote(
            shard_ref.at[which] if own else here, here, sem.at[which, index], recv_sem.at[which, index], **where
        )

    def line_copy(which, index, step, own=False):
        where = {"sec": base + which, "pts": me + 2 * step} if own else {"pts": me + 2 * step}
        return copy(which, index, up_sem if step > 0 else down_sem, own, **where)

    def near_copy(which, index, own=False):
        return copy(which, index, near_sem, own, sec=near)

    def pair_copy(which):
        return copy(which, me, pair_sem, True, sec=base + which, pts=pair)

    def kept(which):
        return pltpu.make_async_copy(shard_ref.at[which], place(which, me), local_sem.at[which])

    swap_to = {"sec": base + side, "pts": spot * 2 + core}

    def swap_rows():
        return remote(points_ref, rows_ref, swap_send.at[0], swap_recv.at[0], **swap_to)

    def swap_aux():
        return remote(aux_ref, rows_aux_ref, swap_send.at[1], swap_recv.at[1], **swap_to)

    def kept_rows():
        return pltpu.make_async_copy(points_ref, rows_ref, local_sem.at[2])

    def kept_aux():
        return pltpu.make_async_copy(aux_ref, rows_aux_ref, local_sem.at[3])

    def query_copy(to):
        return remote(
            points_ref.at[pl.ds(to % 2 * share, share)], query_ref, query_send.at[0, to], query_recv.at[0], sec=to
        )

    def query_aux(to):
        return remote(aux_ref, query_aux_ref, query_send.at[1, to], query_recv.at[1], sec=to)

    def kept_query():
        return pltpu.make_async_copy(points_ref.at[pl.ds(owner % 2 * share, share)], query_ref, local_sem.at[4])

    def kept_query_aux():
        return pltpu.make_async_copy(aux_ref, query_aux_ref, local_sem.at[5])

    @pl.when(core != side)
    def _():
        for which in range(2):
            pair_copy(which).start()

    @pl.when(core == side)
    def _():
        for which in range(2):
            @pl.when(spot < length - 1)
            def _():
                line_copy(which, me, 1, True).start()

            @pl.when(spot > 0)
            def _():
                line_copy(which, me, -1, True).start()

            near_copy(which, me, True).start()
            kept(which).start()

    @pl.when(core != side)
    def _():
        swap_aux().start()
        swap_rows().start()

    @pl.when(core == side)
    def _():
        kept_aux().start()
        kept_rows().start()

    @pl.when(sec == owner)
    def _():
        for to in range(owner):
            query_aux(to).start()
            query_copy(to).start()
        kept_query().start()
        kept_query_aux().start()

    def arrive(index, up, down):
        copy(core, index, near_sem, False, sec=near).wait_recv()
        if up:
            @pl.when(spot < length - 1)
            def _():
                line_copy(core, index, 1).start()
        if down:
            @pl.when(spot > 0)
            def _():
                line_copy(core, index, -1).start()
        near_copy(core, index).start()

    arrive(pair, True, True)
    for distance in range(1, length):
        for other in range(2):
            column = side if other == 0 else 1 - side

            @pl.when(spot - distance >= 0)
            def _():
                arrive((spot - distance) * 2 + column, True, False)

            @pl.when(spot + distance < length)
            def _():
                arrive((spot + distance) * 2 + column, False, True)

    for index in range(blocks):
        @pl.when(index != me)
        def _():
            near_copy(1 - core, index).wait_recv()
            near_copy(core, index).wait_send()

            @pl.when(jnp.logical_and(spot < length - 1, index // 2 <= spot))
            def _():
                line_copy(core, index, 1).wait_send()

            @pl.when(jnp.logical_and(spot > 0, index // 2 >= spot))
            def _():
                line_copy(core, index, -1).wait_send()

    @pl.when(core == side)
    def _():
        for which in range(2):
            @pl.when(spot < length - 1)
            def _():
                line_copy(which, me, 1, True).wait_send()

            @pl.when(spot > 0)
            def _():
                line_copy(which, me, -1, True).wait_send()

            near_copy(which, me, True).wait_send()
            kept(which).wait()
        kept_aux().wait()
        kept_rows().wait()

    @pl.when(core != side)
    def _():
        for which in range(2):
            near_copy(which, me).wait_recv()
            pair_copy(which).wait_send()
        swap_aux().wait()
        swap_rows().wait()

    @pl.when(sec == owner)
    def _():
        for to in range(owner):
            query_aux(to).wait_send()
            query_copy(to).wait_send()
        kept_query().wait()
        kept_query_aux().wait()

    @pl.when(sec != owner)
    def _():
        query_aux(0).wait_recv()
        query_copy(0).wait_recv()


def gather_projections(blocks, sections, shards, points, aux):
    depth, width = shards.shape[1:]
    rows = points.shape[0]
    anywhere = pl.BlockSpec(memory_space=pl.ANY)
    return pl.pallas_call(
        functools.partial(gather_kernel, blocks, sections),
        out_shape=(
            jax.ShapeDtypeStruct((2, depth * blocks, width), shards.dtype),
            jax.ShapeDtypeStruct(points.shape, points.dtype),
            jax.ShapeDtypeStruct(aux.shape, aux.dtype),
            jax.ShapeDtypeStruct((rows // 2, width), points.dtype),
            jax.ShapeDtypeStruct(aux.shape, aux.dtype),
        ),
        in_specs=[anywhere] * 3,
        out_specs=(anywhere,) * 5,
        scratch_shapes=[
            DMA((6,)),
            DMA((2, blocks)),
            DMA((2, blocks)),
            DMA((2, blocks)),
            DMA((2, blocks)),
            DMA((2, blocks)),
            DMA((2,)),
            DMA((2,)),
            DMA((2, sections)),
            DMA((2,)),
        ],
        compiler_params=pltpu.CompilerParams(
            collective_id=0, has_side_effects=True, vmem_limit_bytes=VMEM_LIMIT
        ),
    )(shards, points, aux)


def state_kernel(
    length, part_ref, out_ref, from_near, halves, landed,
    half_send, half_recv, part_send, part_recv, share_send, share_recv, across_send, across_recv,
    pair_send, pair_recv, near_send, near_recv,
):
    sec = lax.axis_index("sec")
    me = lax.axis_index("pts")
    spot, side = me // 2, lax.rem(me, 2)
    core = lax.rem(sec, 2)
    near, across = sibling_of(sec), across_of(sec)
    pair = spot * 2 + 1 - side
    mine = sec - core + side
    beyond = across_of(mine)
    beside = sibling_of(mine)
    corner = across_of(beside)
    barrier = pltpu.get_barrier_semaphore()

    def greet(**where):
        pl.semaphore_signal(barrier, inc=1, device_id=where, device_id_type=MESH)

    def after(step):
        return lax.rem(spot + step, length) * 2 + side

    greet(sec=near)
    greet(sec=across)
    greet(pts=pair)
    for step in range(1, length):
        greet(pts=after(step))
    pl.semaphore_wait(barrier, length + 2)

    half = remote(part_ref.at[1 - core], from_near, half_send, half_recv, sec=near)
    half.start()
    half.wait_recv()
    halves[...] = (part_ref[core].astype(jnp.float32) + from_near[...].astype(jnp.float32)).astype(halves.dtype)

    def part_copy(step):
        return remote(
            halves.at[lax.rem(spot + step, length)], landed.at[step], part_send.at[step], part_recv.at[step],
            pts=after(step),
        )

    def slot(section, step, parity):
        return out_ref.at[section, parity, lax.rem(spot + length - step, length)]

    def share_copy(step):
        here = slot(mine, 0, core)
        return remote(here, here, share_send.at[step], share_recv.at[step], pts=after(step))

    def arriving(step):
        here = slot(mine, step, core)
        return remote(here, here, share_send.at[step], share_recv.at[step], pts=after(step))

    def across_copy(section, step):
        here = slot(section, step, core)
        return remote(here, here, across_send.at[step], across_recv.at[step], sec=across)

    def pair_copy(kind, section, step):
        here = slot(section, step, core)
        return remote(here, here, pair_send.at[kind, step], pair_recv.at[kind, step], pts=pair)

    def near_copy(section, step, parity):
        here = slot(section, step, parity)
        return remote(here, here, near_send.at[section, step], near_recv.at[section, step], sec=near)

    for step in range(1, length):
        part_copy(step).start()
    total = halves[spot].astype(jnp.float32)
    for step in range(1, length):
        part_copy(step).wait_recv()
        total += landed[step].astype(jnp.float32)
    out_ref[mine, core, spot] = total.astype(out_ref.dtype)
    for step in range(1, length):
        share_copy(step).start()
    for step in range(length):
        if step:
            arriving(step).wait_recv()
        across_copy(mine, step).start()
        pair_copy(0, mine, step).start()
        near_copy(mine, step, core).start()
    for step in range(length):
        across_copy(beyond, step).wait_recv()
        pair_copy(1, beyond, step).start()
        near_copy(beyond, step, core).start()
        pair_copy(0, beside, step).wait_recv()
        near_copy(beside, step, core).start()
    for step in range(length):
        pair_copy(1, corner, step).wait_recv()
        near_copy(corner, step, core).start()
    for step in range(length):
        for section in (mine, beyond, beside, corner):
            near_copy(section, step, 1 - core).wait_recv()
    half.wait_send()
    for step in range(1, length):
        part_copy(step).wait_send()
        share_copy(step).wait_send()
    for step in range(length):
        across_copy(mine, step).wait_send()
        pair_copy(0, mine, step).wait_send()
        pair_copy(1, beyond, step).wait_send()
        for section in (mine, beyond, beside, corner):
            near_copy(section, step, core).wait_send()


def sum_states(blocks, sections, parts):
    length = blocks // 2
    inside = pl.BlockSpec(memory_space=pltpu.VMEM)
    slab = parts.shape[1:]
    return pl.pallas_call(
        functools.partial(state_kernel, length),
        out_shape=jax.ShapeDtypeStruct((sections,) + parts.shape, parts.dtype),
        in_specs=[inside],
        out_specs=inside,
        scratch_shapes=[
            pltpu.VMEM(slab, parts.dtype),
            pltpu.VMEM(slab, parts.dtype),
            pltpu.VMEM(slab, parts.dtype),
            DMA,
            DMA,
            DMA((length,)),
            DMA((length,)),
            DMA((length,)),
            DMA((length,)),
            DMA((length,)),
            DMA((length,)),
            DMA((2, length)),
            DMA((2, length)),
            DMA((sections, length)),
            DMA((sections, length)),
        ],
        compiler_params=pltpu.CompilerParams(
            collective_id=1, has_side_effects=True, vmem_limit_bytes=VMEM_LIMIT
        ),
    )(parts)


def feed_kernel(
    centred_ref, mixed_ref, up_ref, down_ref, out_ref,
    rows_in, sums, own, cross, to_near, from_near, to_across, from_across,
    gather_send, gather_recv, near_send, near_recv, across_send, across_recv,
):
    sec = lax.axis_index("sec")
    near, across = sibling_of(sec), across_of(sec)
    core, chip = lax.rem(sec, 2), sec // 2
    share = rows_in.shape[1]
    columns = out_ref.shape[1]
    barrier = pltpu.get_barrier_semaphore()
    for other in (near, across):
        pl.semaphore_signal(barrier, inc=1, device_id={"sec": other}, device_id_type=MESH)
    pl.semaphore_wait(barrier, 2)

    def near_rows(index):
        return remote(
            centred_ref.at[pl.ds(index * share, share)], rows_in.at[index], gather_send.at[index],
            gather_recv.at[index], sec=near,
        )

    def near_copy(block):
        return remote(to_near.at[block], from_near.at[block], near_send.at[block], near_recv.at[block], sec=near)

    def across_copy(block):
        return remote(
            to_across.at[block], from_across.at[block], across_send.at[block], across_recv.at[block], sec=across
        )

    for index in range(2):
        near_rows(index).start()
    span = 256
    steps = up_ref.shape[1] // span

    def side_of(which):
        return pl.ds(pl.multiple_of(which * 2 * columns, 2 * columns), 2 * columns)

    def run(source):
        @pl.loop(0, steps)
        def _(step):
            units = pl.ds(pl.multiple_of(step * span, span), span)
            hidden = jax.nn.gelu(
                jnp.dot(source[...], up_ref[:, units], preferred_element_type=jnp.float32), approximate=True
            ).astype(jnp.bfloat16)
            sums[...] += jnp.dot(hidden, down_ref[units, :], preferred_element_type=jnp.float32)

    def part(of):
        return sums[:, pl.ds(pl.multiple_of(of * columns, columns), columns)]

    def emit(block):
        own[block] = part(sec)
        cross[block] = part(across)
        to_near[block, 0] = part(1 - core).astype(jnp.bfloat16)
        to_near[block, 1] = part(3 - core).astype(jnp.bfloat16)
        near_copy(block).start()

    def forward(block):
        near_copy(block).wait_recv()
        to_across[block] = (cross[block] + from_near[block, 1 - chip].astype(jnp.float32)).astype(jnp.bfloat16)
        across_copy(block).start()

    order = []
    for index in range(2):
        mine, theirs = core * 2 + index, (1 - core) * 2 + index
        rows = pl.ds(index * share, share)
        sums[:, side_of(chip)] = mixed_ref[rows, side_of(chip)]
        sums[:, side_of(1 - chip)] = jnp.zeros((share, 2 * columns), jnp.float32)
        run(centred_ref.at[rows])
        emit(mine)
        near_rows(index).wait_recv()
        sums[...] = jnp.zeros_like(sums)
        run(rows_in.at[index])
        emit(theirs)
        forward(theirs)
        forward(mine)
        order += [theirs, mine]
    for block in order:
        across_copy(block).wait_recv()
        out_ref[pl.ds(pl.multiple_of(block * share, share), share), :] = (
            own[block] + from_near[block, chip].astype(jnp.float32) + from_across[block].astype(jnp.float32)
        ).astype(out_ref.dtype)
    for block in order:
        near_copy(block).wait_send()
        across_copy(block).wait_send()
    for index in range(2):
        near_rows(index).wait_send()


def feed_forward(sections, centred, mixed, up, down):
    width = centred.shape[1]
    share = centred.shape[0] // 2
    columns = width // sections
    inside = pl.BlockSpec(memory_space=pltpu.VMEM)
    half = jnp.bfloat16
    return pl.pallas_call(
        feed_kernel,
        out_shape=jax.ShapeDtypeStruct((share * 4, columns), half),
        in_specs=[inside] * 4,
        out_specs=inside,
        scratch_shapes=[
            pltpu.VMEM((2, share, width), half),
            pltpu.VMEM((share, width), jnp.float32),
            pltpu.VMEM((4, share, columns), jnp.float32),
            pltpu.VMEM((4, share, columns), jnp.float32),
            pltpu.VMEM((4, 2, share, columns), half),
            pltpu.VMEM((4, 2, share, columns), half),
            pltpu.VMEM((4, share, columns), half),
            pltpu.VMEM((4, share, columns), half),
            DMA((2,)),
            DMA((2,)),
            DMA((4,)),
            DMA((4,)),
            DMA((4,)),
            DMA((4,)),
        ],
        compiler_params=pltpu.CompilerParams(
            collective_id=2, has_side_effects=True, vmem_limit_bytes=VMEM_LIMIT
        ),
    )(centred, mixed, up, down)


def on_device(
    points,
    counts,
    input_gain,
    key_weight,
    value_weight,
    query_weight,
    output_weight,
    middle_gain,
    up_weight,
    down_weight,
):
    block = points[0]
    rows, width = block.shape
    heads = width // HEAD_DIM
    sections = lax.axis_size("sec")
    blocks = lax.axis_size("pts")
    aux = jnp.concatenate(
        [
            input_gain.reshape(heads, HEAD_DIM),
            jnp.broadcast_to(counts.astype(jnp.float32), (heads, HEAD_DIM)),
        ]
    )
    whole, taken, taken_aux, query_rows, query_aux = gather_projections(
        blocks, sections, jnp.concatenate([key_weight, value_weight]), block, aux
    )
    whole_key, whole_value = whole[0], whole[1]
    query_gain = query_aux[:heads]
    normed = layer_normalizer(
        taken.astype(jnp.float32), taken_aux[:heads].reshape(width)
    ).astype(jnp.bfloat16)
    valid = jnp.arange(rows).astype(jnp.float32) < taken_aux[heads, 0]
    key_feats = feature_map(
        jnp.dot(normed, whole_key, preferred_element_type=jnp.float32)
    ).astype(jnp.bfloat16)
    key_feats = jnp.where(valid[:, None], key_feats, jnp.zeros_like(key_feats))
    value_rows = jnp.dot(normed, whole_value, preferred_element_type=jnp.float32).astype(jnp.bfloat16)
    local_state = jnp.einsum(
        "yzl,yzn->zln",
        key_feats.reshape(rows, heads, HEAD_DIM),
        value_rows.reshape(rows, heads, HEAD_DIM),
        preferred_element_type=jnp.float32,
    ).reshape(width, HEAD_DIM)
    local_total = jnp.sum(key_feats.astype(jnp.float32), axis=0)
    slab = width // blocks
    extra = jnp.pad(local_total.reshape(blocks, 1, slab), ((0, 0), (0, EXTRA - 1), (0, HEAD_DIM - slab)))
    parts = jnp.concatenate([local_state.reshape(blocks, slab, HEAD_DIM), extra], axis=1).astype(jnp.bfloat16)
    summed = sum_states(blocks, sections, parts.reshape((2, blocks // 2) + parts.shape[1:]))
    summed = summed.reshape((sections,) + parts.shape)
    state_heads = summed[:, :, :slab].reshape(sections, heads, HEAD_DIM, HEAD_DIM)
    total_heads = summed[:, :, slab, :slab].reshape(sections, heads, HEAD_DIM)

    query_wide = query_rows.astype(jnp.float32)
    query_normed = layer_normalizer(query_wide, query_gain.reshape(width)).astype(jnp.bfloat16)
    query_feats = feature_map(
        jnp.dot(query_normed, query_weight, preferred_element_type=jnp.float32)
    ).astype(jnp.bfloat16)
    share = query_rows.shape[0]
    per_head_queries = query_feats.reshape(share, heads, HEAD_DIM)
    numerator = jnp.einsum(
        "rhk,shkv->srhv", per_head_queries, state_heads, preferred_element_type=jnp.float32
    )
    denom = jnp.einsum("rhk,shk->srh", per_head_queries, total_heads, preferred_element_type=jnp.float32)
    attended = (
        jnp.sum(numerator / denom[:, :, :, None], axis=0).reshape(share, width).astype(jnp.bfloat16)
    )
    mixed = query_wide + jnp.dot(attended, output_weight, preferred_element_type=jnp.float32)
    centred = layer_normalizer(mixed, middle_gain).astype(jnp.bfloat16)
    return feed_forward(sections, centred, mixed, up_weight, down_weight)


def solution(mesh):
    placed = (
        P("sec", "pts", None),
        P("sec", "pts"),
        P("sec", None),
        P("sec", "pts", None),
        P("sec", "pts", None),
        P(),
        P(),
        P(),
        P(None, "sec"),
        P("sec", None),
    )
    return jax.shard_map(
        on_device, mesh=mesh, in_specs=placed, out_specs=P("pts", "sec"), check_vma=False
    )
```

time: 124 us -> 114 us (0.919)
  Pallas kernels: 105 us -> 89.3 us
  other arithmetic: 2 us -> 4.28 us
  matrix products: 11.6 us -> 13.7 us
    pallas_call x1, Pallas kernels: 52.4 us -> 42.7 us  [gather_projections(): pl.pallas_call(functools.partial(gather_kernel, blocks, sections), out_sh...]
    pallas_call x2, Pallas kernels: 52.4 us -> 46.6 us  [the longest x1 25.3 us: feed_forward(): pl.pallas_call(feed_kernel, out_shape=jax.ShapeDtypeStruct((share * 4, co...]
    unnamed x18 -> x15, local copies, waits for them, and re-layouts: 4.77 us -> 3.93 us
where the time goes in v2:
time: 114 us; the launch traced here: 113 us
  Pallas kernels  89.3 us (78%)
  matrix products  13.7 us (12%)
  local copies, waits for them, and re-layouts  5.16 us (5%)
  other arithmetic  4.28 us (4%)
    pallas_call x1, Pallas kernels, gather_projections(): pl.pallas_call(functools.partial(gather_kernel, blocks, sections), out_sh...  42.7 us
    pallas_call x1, Pallas kernels, feed_forward(): pl.pallas_call(feed_kernel, out_shape=jax.ShapeDtypeStruct((share * 4, co...  25.3 us
    pallas_call x1, Pallas kernels, sum_states(): pl.pallas_call(functools.partial(state_kernel, length), out_shape=jax.Sha...  21.4 us
    dot_general x1, matrix products, on_device(): jnp.dot(normed, whole_key, preferred_element_type=jnp.float32)  5.18 us
    unnamed x15, local copies, waits for them, and re-layouts  3.93 us
    dot_general x1, matrix products, on_device(): jnp.dot(normed, whole_value, preferred_element_type=jnp.float32)  2.82 us

profile of v2, /device:TPU:0, one launch (start us, length us, event | category | flops | bytes accessed | tf_op | source)
XLA Modules:
  0.0 113.3 jit_solution(337623529814720290)
XLA Ops:
  0.0 0.0 copy-start
  0.0 1.2 %pad_maximum_fusion.shard_ref = bf16[2,128,1024]{2,1,0:T(8,128)(2,1)S(1)} fusion(bf16[1,128,1024]{2,1,0:T(8,128)(2,1)} %param.14, bf16[1,128,1024]{2,1,0:T(8,128)(2,1)} %param.13), kind=kLoop, calls=%fused_computation.47 | loop fusion | flops 262144 | bytes 1048576 | tf_op jit(solution)/shard_map/concatenate | solution.py:555
  1.9 0.7 concatenate.16.aux_ref
  2.6 0.0 copy-start.1
  2.6 1.6 %copy-done.1 = bf16[1,1024,1024]{2,1,0:T(8,128)(2,1)S(1)} copy-done((bf16[1,1024,1024]{2,1,0:T(8,128)(2,1)S(1)}, bf16[1,1024,1024]{2,1,0:T(8,128)(2,1)}, u32[]{:S(2)}) %copy-start.1) | copy-done | bytes 2097176
  4.2 42.7 %shard_map.100 = (bf16[2,1024,1024]{2,1,0:T(8,128)(2,1)}, bf16[1024,1024]{1,0:T(8,128)(2,1)S(1)}, f32[16,128]{1,0:T(8,128)S(1)}, bf16[512,1024]{1,0:T(8,128)(2,1)S(1)}, f32[16,128]{1,0:T(8,128)S(1)}) custom-call(bf16[2,128,1024]{2,1,0:T(8,128)(2,1)S(1)} %pad_maximum_fusion.shard_ref, bf16[1024,1024]{1,0:T(8,128)(2,1)S(1)} %bitcast.52, ...), custom_call_target="tpu_custom_call" | custom-call | tf_op jit(solution)/shard_map/pallas_call | solution.py:246
  46.8 0.0 copy-start.4
  46.8 0.3 convert_reduce_fusion
  47.2 0.7 fusion.3
  47.9 0.5 slice.21
  48.4 0.7 convert_compare_fusion
  49.1 0.0 copy-done.4
  49.1 5.2 %fusion.42 = (bf16[1024]{0:T(1024)(128)(2,1)S(1)}, bf16[1024,1024]{0,1:T(8,128)(2,1)S(1)}) fusion(bf16[2,1024,1024]{2,1,0:T(8,128)(2,1)S(1)} %copy-done.4, bf16[1024,1024]{1,0:T(8,128)(2,1)S(1)} %get-tuple-element.12, f32[1024]{0:T(1024)S(1)} %get-tuple-element.20, f32[1024]{0:T(1024)S(1)} %add_rsqrt_fusion, f32[1024]{0:T(1024)S(1)} %broadcast_multiply_fusion, ...), kind=kOutput, calls=%fused_computation.59 | convolution fusion | flops 2160065536 | bytes 6306816 | tf_op jit(solution)/shard_map/dot_general | solution.py:564
  54.3 2.8 %fusion.24 = bf16[1024,1024]{0,1:T(8,128)(2,1)S(1)} fusion(bf16[2,1024,1024]{2,1,0:T(8,128)(2,1)S(1)} %copy-done.4, bf16[1024,1024]{1,0:T(8,128)(2,1)S(1)} %get-tuple-element.12, f32[1024]{0:T(1024)S(1)} %get-tuple-element.20, f32[1024]{0:T(1024)S(1)} %add_rsqrt_fusion, f32[1024]{0:T(1024)S(1)} %broadcast_multiply_fusion), kind=kOutput, calls=%fused_computation.36 | convolution fusion | flops 2153775104 | bytes 6303744 | tf_op jit(solution)/shard_map/dot_general | solution.py:567
  57.1 0.7 convolution_convert_fusion
  57.9 0.0 copy-start.5
  57.9 21.4 %shard_map.101 = bf16[4,2,4,144,128]{4,3,2,1,0:T(8,128)(2,1)S(1)} custom-call(bf16[2,4,144,128]{3,2,1,0:T(8,128)(2,1)S(1)} %pad_maximum_fusion.1.part_ref), custom_call_target="tpu_custom_call" | custom-call | tf_op jit(solution)/shard_map/pallas_call | solution.py:382
  79.3 0.2 convert_reduce_fusion.1
  79.5 0.4 fusion.11
  79.9 0.0 copy-done.5
  79.9 1.9 %fusion.17 = bf16[512,1024]{1,0:T(8,128)(2,1)S(1)} fusion(bf16[1024,1024]{1,0:T(8,128)(2,1)S(1)} %copy-done.5, bf16[512,1024]{1,0:T(8,128)(2,1)S(1)} %get-tuple-element.10, f32[1024]{0:T(1024)S(1)} %get-tuple-element.19, f32[512]{0:T(512)S(1)} %add_rsqrt_fusion.2, f32[512]{0:T(512)S(1)} %broadcast_multiply_fusion.2), kind=kOutput, calls=%fused_computation.27 | convolution fusion | flops 1078984704 | bytes 4202496 | tf_op jit(solution)/shard_map/dot_general | solution.py:586
  81.9 0.4 convolution_bitcast_fusion
  82.2 0.3 copy.36
  82.5 1.3 %fusion = bf16[512,8,128]{0,2,1:T(8,128)(2,1)S(1)} fusion(f32[4,512,8]{1,0,2:T(4,128)S(1)} %convolution_bitcast_fusion, bf16[512,8,128,1]{2,1,0,3:T(8,128)(2,1)S(1)} %bitcast.59, bf16[4,8,144,128]{3,2,1,0:T(8,128)(2,1)S(1)} %bitcast.54), kind=kOutput, calls=%fused_computation.3 | convolution fusion | flops 540540928 | bytes 3211264 | tf_op jit(solution)/shard_map/rhk,shkv->srhv/dot_general | solution.py:590
  83.9 0.0 copy-done
  83.9 1.4 %fusion.43 = (f32[512]{0:T(512)S(1)}, f32[512,1024]{1,0:T(8,128)S(1)}) fusion(bf16[512,1024]{0,1:T(8,128)(2,1)S(1)} %bitcast.60, bf16[1024,1024]{1,0:T(8,128)(2,1)S(1)} %copy-done, bf16[512,1024]{1,0:T(8,128)(2,1)S(1)} %get-tuple-element.10), kind=kOutput, calls=%fused_computation.60 | convolution fusion | flops 1075314176 | bytes 6293504 | tf_op jit(solution)/shard_map/dot_general | solution.py:597
  85.3 0.3 multiply_reduce_fusion
  85.6 0.3 copy-done.3
  85.9 0.3 multiply_convert_fusion.centred_ref
  86.3 0.9 copy-done.2
  87.2 25.3 %shard_map.102 = bf16[1024,256]{1,0:T(8,128)(2,1)S(1)} custom-call(bf16[512,1024]{1,0:T(8,128)(2,1)S(1)} %multiply_convert_fusion.centred_ref, f32[512,1024]{1,0:T(8,128)S(1)} %get-tuple-element.18.mixed_ref, bf16[1024,1024]{1,0:T(8,128)(2,1)S(1)} %copy-done.2, bf16[1024,1024]{1,0:T(8,128)(2,1)} %down_ref.1), custom_call_target="tpu_custom_call" | custom-call | tf_op jit(solution)/shard_map/pallas_call | solution.py:504
  112.5 0.8 copy.49
  (13 shorter events, 0.1 us)
Async XLA Ops:
  0.0 83.9 %copy-start = (bf16[1024,1024]{1,0:T(8,128)(2,1)S(1)}, bf16[1024,1024]{1,0:T(8,128)(2,1)}, u32[]{:S(2)}) copy-start(bf16[1024,1024]{1,0:T(8,128)(2,1)} %param.16) | copy-start | bytes 6291460
  2.6 1.6 %copy-start.1 = (bf16[1,1024,1024]{2,1,0:T(8,128)(2,1)S(1)}, bf16[1,1024,1024]{2,1,0:T(8,128)(2,1)}, u32[]{:S(2)}) copy-start(bf16[1,1024,1024]{2,1,0:T(8,128)(2,1)} %param.10) | copy-start | bytes 6291460
  46.8 2.3 %copy-start.4 = (bf16[2,1024,1024]{2,1,0:T(8,128)(2,1)S(1)}, bf16[2,1024,1024]{2,1,0:T(8,128)(2,1)}, u32[]{:S(2)}) copy-start(bf16[2,1024,1024]{2,1,0:T(8,128)(2,1)} %get-tuple-element.13) | copy-start | bytes 12582916
  57.9 22.1 %copy-start.5 = (bf16[1024,1024]{1,0:T(8,128)(2,1)S(1)}, bf16[1024,1024]{1,0:T(8,128)(2,1)}, u32[]{:S(2)}) copy-start(bf16[1024,1024]{1,0:T(8,128)(2,1)} %param.15) | copy-start | bytes 6291460
  85.2 0.7 copy-start.3
  85.6 1.6 %copy-start.2 = (bf16[1024,1024]{1,0:T(8,128)(2,1)S(1)}, bf16[1024,1024]{1,0:T(8,128)(2,1)}, u32[]{:S(2)}) copy-start(bf16[1024,1024]{1,0:T(8,128)(2,1)} %up_ref.1) | copy-start | bytes 6291460

commit v3 on v2

--- a/solution.py
+++ b/solution.py
@@ -45,12 +45,13 @@
 
 
 def gather_kernel(
-    blocks, sections, shard_ref, points_ref, aux_ref,
+    blocks, sections, key_ref, value_ref, points_ref, aux_ref,
     whole_ref, rows_ref, rows_aux_ref, query_ref, query_aux_ref,
     local_sem, up_sem, down_sem, near_sem, pair_sem, recv_sem, swap_send, swap_recv, query_send, query_recv,
 ):
     length = blocks // 2
-    depth = shard_ref.shape[1]
+    shards = (key_ref, value_ref)
+    depth = key_ref.shape[0]
     share = query_ref.shape[0]
     sec = lax.axis_index("sec")
     me = lax.axis_index("pts")
@@ -81,7 +82,7 @@
     def copy(which, index, sem, own, **where):
         here = place(which, index)
         return remote(
-            shard_ref.at[which] if own else here, here, sem.at[which, index], recv_sem.at[which, index], **where
+            shards[which] if own else here, here, sem.at[which, index], recv_sem.at[which, index], **where
         )
 
     def line_copy(which, index, step, own=False):
@@ -95,7 +96,7 @@
         return copy(which, me, pair_sem, True, sec=base + which, pts=pair)
 
     def kept(which):
-        return pltpu.make_async_copy(shard_ref.at[which], place(which, me), local_sem.at[which])
+        return pltpu.make_async_copy(shards[which], place(which, me), local_sem.at[which])
 
     swap_to = {"sec": base + side, "pts": spot * 2 + core}
 
@@ -143,11 +144,6 @@
 
             near_copy(which, me, True).start()
             kept(which).start()
-
-    @pl.when(core != side)
-    def _():
-        swap_aux().start()
-        swap_rows().start()
 
     @pl.when(core == side)
     def _():
@@ -162,6 +158,13 @@
         kept_query().start()
         kept_query_aux().start()
 
+    @pl.when(core != side)
+    def _():
+        for which in range(2):
+            pair_copy(which).wait_send()
+        swap_aux().start()
+        swap_rows().start()
+
     def arrive(index, up, down):
         copy(core, index, near_sem, False, sec=near).wait_recv()
         if up:
@@ -221,7 +224,6 @@
     def _():
         for which in range(2):
             near_copy(which, me).wait_recv()
-            pair_copy(which).wait_send()
         swap_aux().wait()
         swap_rows().wait()
 
@@ -239,20 +241,20 @@
         query_copy(0).wait_recv()
 
 
-def gather_projections(blocks, sections, shards, points, aux):
-    depth, width = shards.shape[1:]
+def gather_projections(blocks, sections, key, value, points, aux):
+    depth, width = key.shape
     rows = points.shape[0]
     anywhere = pl.BlockSpec(memory_space=pl.ANY)
     return pl.pallas_call(
         functools.partial(gather_kernel, blocks, sections),
         out_shape=(
-            jax.ShapeDtypeStruct((2, depth * blocks, width), shards.dtype),
+            jax.ShapeDtypeStruct((2, depth * blocks, width), key.dtype),
             jax.ShapeDtypeStruct(points.shape, points.dtype),
             jax.ShapeDtypeStruct(aux.shape, aux.dtype),
             jax.ShapeDtypeStruct((rows // 2, width), points.dtype),
             jax.ShapeDtypeStruct(aux.shape, aux.dtype),
         ),
-        in_specs=[anywhere] * 3,
+        in_specs=[anywhere] * 4,
         out_specs=(anywhere,) * 5,
         scratch_shapes=[
             DMA((6,)),
@@ -266,10 +268,8 @@
             DMA((2, sections)),
             DMA((2,)),
         ],
-        compiler_params=pltpu.CompilerParams(
-            collective_id=0, has_side_effects=True, vmem_limit_bytes=VMEM_LIMIT
-        ),
-    )(shards, points, aux)
+        compiler_params=pltpu.CompilerParams(collective_id=0, has_side_effects=True),
+    )(key, value, points, aux)
 
 
 def state_kernel(
@@ -409,7 +409,7 @@
 
 def feed_kernel(
     centred_ref, mixed_ref, up_ref, down_ref, out_ref,
-    rows_in, sums, own, cross, to_near, from_near, to_across, from_across,
+    rows_in, hidden, sums, own, cross, to_near, from_near, to_across, from_across,
     gather_send, gather_recv, near_send, near_recv, across_send, across_recv,
 ):
     sec = lax.axis_index("sec")
@@ -438,20 +438,19 @@
 
     for index in range(2):
         near_rows(index).start()
-    span = 256
-    steps = up_ref.shape[1] // span
+    span = 512
+    spans = [pl.ds(start, span) for start in range(0, up_ref.shape[1], span)]
 
     def side_of(which):
         return pl.ds(pl.multiple_of(which * 2 * columns, 2 * columns), 2 * columns)
 
     def run(source):
-        @pl.loop(0, steps)
-        def _(step):
-            units = pl.ds(pl.multiple_of(step * span, span), span)
-            hidden = jax.nn.gelu(
+        for units in spans:
+            hidden[:, units] = jax.nn.gelu(
                 jnp.dot(source[...], up_ref[:, units], preferred_element_type=jnp.float32), approximate=True
-            ).astype(jnp.bfloat16)
-            sums[...] += jnp.dot(hidden, down_ref[units, :], preferred_element_type=jnp.float32)
+            ).astype(hidden.dtype)
+        for outs in spans:
+            sums[:, outs] = jnp.dot(hidden[...], down_ref[:, outs], preferred_element_type=jnp.float32)
 
     def part(of):
         return sums[:, pl.ds(pl.multiple_of(of * columns, columns), columns)]
@@ -472,12 +471,10 @@
     for index in range(2):
         mine, theirs = core * 2 + index, (1 - core) * 2 + index
         rows = pl.ds(index * share, share)
-        sums[:, side_of(chip)] = mixed_ref[rows, side_of(chip)]
-        sums[:, side_of(1 - chip)] = jnp.zeros((share, 2 * columns), jnp.float32)
         run(centred_ref.at[rows])
+        sums[:, side_of(chip)] += mixed_ref[rows, side_of(chip)]
         emit(mine)
         near_rows(index).wait_recv()
-        sums[...] = jnp.zeros_like(sums)
         run(rows_in.at[index])
         emit(theirs)
         forward(theirs)
@@ -508,6 +505,7 @@
         out_specs=inside,
         scratch_shapes=[
             pltpu.VMEM((2, share, width), half),
+            pltpu.VMEM((share, up.shape[1]), half),
             pltpu.VMEM((share, width), jnp.float32),
             pltpu.VMEM((4, share, columns), jnp.float32),
             pltpu.VMEM((4, share, columns), jnp.float32),
@@ -552,7 +550,7 @@
         ]
     )
     whole, taken, taken_aux, query_rows, query_aux = gather_projections(
-        blocks, sections, jnp.concatenate([key_weight, value_weight]), block, aux
+        blocks, sections, key_weight[0], value_weight[0], block, aux
     )
     whole_key, whole_value = whole[0], whole[1]
     query_gain = query_aux[:heads]

time: 114 us -> 184 us (1.61)
  Pallas kernels: 89.3 us -> 159 us
    pallas_call x1, Pallas kernels: 42.7 us -> 86.7 us  [gather_projections(): pl.pallas_call(functools.partial(gather_kernel, blocks, sections), out_sh...]
    pallas_call x1, Pallas kernels: 21.4 us -> 52.2 us  [sum_states(): pl.pallas_call(functools.partial(state_kernel, length), out_shape=jax.Sha...]
    pallas_call x1, Pallas kernels: 25.3 us -> 19.7 us  [feed_forward(): pl.pallas_call(feed_kernel, out_shape=jax.ShapeDtypeStruct((share * 4, co...]
    unnamed x15 -> x21, local copies, waits for them, and re-layouts: 3.93 us -> 2.47 us
where the time goes in v3:
time: 184 us
  Pallas kernels  159 us (86%)
  matrix products  15.4 us (8%)
  other arithmetic  4.78 us (3%)
  local copies, waits for them, and re-layouts  4.29 us (2%)
    pallas_call x1, Pallas kernels, gather_projections(): pl.pallas_call(functools.partial(gather_kernel, blocks, sections), out_sh...  86.7 us
    pallas_call x1, Pallas kernels, sum_states(): pl.pallas_call(functools.partial(state_kernel, length), out_shape=jax.Sha...  52.2 us
    pallas_call x1, Pallas kernels, feed_forward(): pl.pallas_call(feed_kernel, out_shape=jax.ShapeDtypeStruct((share * 4, co...  19.7 us
    dot_general x1, matrix products, on_device(): jnp.dot(normed, whole_key, preferred_element_type=jnp.float32)  6.85 us

profile of v3, /device:TPU:0, one launch (start us, length us, event | category | flops | bytes accessed | tf_op | source)
XLA Modules:
  0.0 184.2 jit_solution(2080042465908417880)
XLA Ops:
  0.0 0.0 copy-start
  0.8 1.3 concatenate.12.aux_ref
  2.1 86.7 %shard_map.100 = (bf16[2,1024,1024]{2,1,0:T(8,128)(2,1)}, bf16[1024,1024]{1,0:T(8,128)(2,1)}, f32[16,128]{1,0:T(8,128)}, bf16[512,1024]{1,0:T(8,128)(2,1)}, f32[16,128]{1,0:T(8,128)}) custom-call(bf16[128,1024]{1,0:T(8,128)(2,1)} %bitcast.63, bf16[128,1024]{1,0:T(8,128)(2,1)} %bitcast.64, bf16[1024,1024]{1,0:T(8,128)(2,1)} %bitcast.57, ...), custom_call_target="tpu_custom_call" | custom-call | tf_op jit(solution)/shard_map/pallas_call | solution.py:248
  88.8 0.0 copy-start.3
  88.8 0.0 copy-start.5
  88.8 0.0 copy-start.6
  88.8 2.1 %convert_reduce_fusion = f32[1024]{0:T(1024)S(1)} fusion(bf16[1024,1024]{1,0:T(8,128)(2,1)} %get-tuple-element.12), kind=kLoop, calls=%fused_computation.7 | loop fusion | flops 2096128 | bytes 2101248 | tf_op jit(solution)/shard_map/reduce_sum | solution.py:18
  90.9 0.1 copy-done.3
  91.0 0.7 fusion.3
  91.7 0.0 copy-done.5
  91.7 0.0 copy-done.6
  91.8 0.5 slice.21
  92.3 0.7 convert_compare_fusion
  92.9 6.9 %fusion.42 = (bf16[1024]{0:T(1024)(128)(2,1)S(1)}, bf16[1024,1024]{0,1:T(8,128)(2,1)S(1)}) fusion(bf16[2,1024,1024]{2,1,0:T(8,128)(2,1)} %get-tuple-element.13, bf16[1024,1024]{1,0:T(8,128)(2,1)S(1)} %copy-done.3, f32[1024]{0:T(1024)S(1)} %get-tuple-element.20, f32[1024]{0:T(1024)S(1)} %add_rsqrt_fusion, f32[1024]{0:T(1024)S(1)} %broadcast_multiply_fusion, ...), kind=kOutput, calls=%fused_computation.58 | convolution fusion | flops 2160065536 | bytes 6306816 | tf_op jit(solution)/shard_map/dot_general | solution.py:562
  99.8 2.8 %fusion.24 = bf16[1024,1024]{0,1:T(8,128)(2,1)S(1)} fusion(bf16[2,1024,1024]{2,1,0:T(8,128)(2,1)S(1)} %copy-done.7, bf16[1024,1024]{1,0:T(8,128)(2,1)S(1)} %copy-done.3, f32[1024]{0:T(1024)S(1)} %get-tuple-element.20, f32[1024]{0:T(1024)S(1)} %add_rsqrt_fusion, f32[1024]{0:T(1024)S(1)} %broadcast_multiply_fusion), kind=kOutput, calls=%fused_computation.36 | convolution fusion | flops 2153775104 | bytes 6303744 | tf_op jit(solution)/shard_map/dot_general | solution.py:565
  102.6 0.7 convolution_convert_fusion
  103.4 0.0 copy-start.8
  103.4 52.2 %shard_map.101 = bf16[4,2,4,144,128]{4,3,2,1,0:T(8,128)(2,1)S(1)} custom-call(bf16[2,4,144,128]{3,2,1,0:T(8,128)(2,1)S(1)} %pad_maximum_fusion.part_ref), custom_call_target="tpu_custom_call" | custom-call | tf_op jit(solution)/shard_map/pallas_call | solution.py:382
  155.6 0.2 convert_reduce_fusion.1
  155.9 0.4 fusion.11
  156.3 0.0 copy-done.8
  156.3 1.9 %fusion.17 = bf16[512,1024]{1,0:T(8,128)(2,1)S(1)} fusion(bf16[1024,1024]{1,0:T(8,128)(2,1)S(1)} %copy-done.8, bf16[512,1024]{1,0:T(8,128)(2,1)S(1)} %copy-done.2, f32[1024]{0:T(1024)S(1)} %get-tuple-element.19, f32[512]{0:T(512)S(1)} %add_rsqrt_fusion.2, f32[512]{0:T(512)S(1)} %broadcast_multiply_fusion.2), kind=kOutput, calls=%fused_computation.27 | convolution fusion | flops 1078984704 | bytes 4202496 | tf_op jit(solution)/shard_map/dot_general | solution.py:584
  158.2 0.4 convolution_bitcast_fusion
  158.6 0.3 copy.36
  158.9 1.4 fusion
  160.3 1.4 fusion.43
  161.7 0.3 multiply_reduce_fusion
  162.0 0.3 copy-done.4
  162.4 0.3 multiply_convert_fusion.centred_ref
  162.7 0.9 copy-done.1
  163.6 19.7 %shard_map.102 = bf16[1024,256]{1,0:T(8,128)(2,1)S(1)} custom-call(bf16[512,1024]{1,0:T(8,128)(2,1)S(1)} %multiply_convert_fusion.centred_ref, f32[512,1024]{1,0:T(8,128)S(1)} %get-tuple-element.18.mixed_ref, bf16[1024,1024]{1,0:T(8,128)(2,1)S(1)} %copy-done.1, bf16[1024,1024]{1,0:T(8,128)(2,1)} %down_ref.1), custom_call_target="tpu_custom_call" | custom-call | tf_op jit(solution)/shard_map/pallas_call | solution.py:501
  183.4 0.8 copy.49
  (18 shorter events, 0.1 us)
Async XLA Ops:
  0.0 160.3 %copy-start = (bf16[1024,1024]{1,0:T(8,128)(2,1)S(1)}, bf16[1024,1024]{1,0:T(8,128)(2,1)}, u32[]{:S(2)}) copy-start(bf16[1024,1024]{1,0:T(8,128)(2,1)} %param.16) | copy-start | bytes 6291460
  88.8 2.2 %copy-start.3 = (bf16[1024,1024]{1,0:T(8,128)(2,1)S(1)}, bf16[1024,1024]{1,0:T(8,128)(2,1)}, u32[]{:S(2)}) copy-start(bf16[1024,1024]{1,0:T(8,128)(2,1)} %get-tuple-element.12) | copy-start | bytes 6291460
  88.8 2.9 %copy-start.5 = (f32[16,128]{1,0:T(8,128)S(1)}, f32[16,128]{1,0:T(8,128)}, u32[]{:S(2)}) copy-start(f32[16,128]{1,0:T(8,128)} %get-tuple-element.11) | copy-start | bytes 24580
  88.8 2.9 %copy-start.6 = (f32[16,128]{1,0:T(8,128)S(1)}, f32[16,128]{1,0:T(8,128)}, u32[]{:S(2)}) copy-start(f32[16,128]{1,0:T(8,128)} %get-tuple-element.14) | copy-start | bytes 24580
  92.9 6.9 %copy-start.7 = (bf16[2,1024,1024]{2,1,0:T(8,128)(2,1)S(1)}, bf16[2,1024,1024]{2,1,0:T(8,128)(2,1)}, u32[]{:S(2)}) copy-start(bf16[2,1024,1024]{2,1,0:T(8,128)(2,1)} %get-tuple-element.13) | copy-start | bytes 12582916
  103.3 52.3 %copy-start.2 = (bf16[512,1024]{1,0:T(8,128)(2,1)S(1)}, bf16[512,1024]{1,0:T(8,128)(2,1)}, u32[]{:S(2)}) copy-start(bf16[512,1024]{1,0:T(8,128)(2,1)} %get-tuple-element.10) | copy-start | bytes 3145732
  103.4 52.9 %copy-start.8 = (bf16[1024,1024]{1,0:T(8,128)(2,1)S(1)}, bf16[1024,1024]{1,0:T(8,128)(2,1)}, u32[]{:S(2)}) copy-start(bf16[1024,1024]{1,0:T(8,128)(2,1)} %param.15) | copy-start | bytes 6291460
  161.7 0.7 copy-start.4
  162.0 1.6 copy-start.1

commit v4 on v3

--- a/solution.py
+++ b/solution.py
@@ -268,7 +268,9 @@
             DMA((2, sections)),
             DMA((2,)),
         ],
-        compiler_params=pltpu.CompilerParams(collective_id=0, has_side_effects=True),
+        compiler_params=pltpu.CompilerParams(
+            collective_id=0, has_side_effects=True, vmem_limit_bytes=VMEM_LIMIT
+        ),
     )(key, value, points, aux)
 
 

time: 184 us -> 111 us (0.60)
  Pallas kernels: 159 us -> 85.6 us
  local copies, waits for them, and re-layouts: 4.29 us -> 7.06 us
    pallas_call x1, Pallas kernels: 86.7 us -> 42.7 us  [gather_projections(): pl.pallas_call(functools.partial(gather_kernel, blocks, sections), out_sh...]
    pallas_call x1, Pallas kernels: 52.2 us -> 23.2 us  [sum_states(): pl.pallas_call(functools.partial(state_kernel, length), out_shape=jax.Sha...]
    unnamed x21 -> x19, local copies, waits for them, and re-layouts: 2.47 us -> 5.83 us
where the time goes in v4:
time: 111 us; the launch traced here: 110 us
  Pallas kernels  85.6 us (77%)
  matrix products  13.7 us (12%)
  local copies, waits for them, and re-layouts  7.06 us (6%)
  other arithmetic  3.05 us (3%)
    pallas_call x1, Pallas kernels, gather_projections(): pl.pallas_call(functools.partial(gather_kernel, blocks, sections), out_sh...  42.7 us
    pallas_call x1, Pallas kernels, sum_states(): pl.pallas_call(functools.partial(state_kernel, length), out_shape=jax.Sha...  23.2 us
    pallas_call x1, Pallas kernels, feed_forward(): pl.pallas_call(feed_kernel, out_shape=jax.ShapeDtypeStruct((share * 4, co...  19.7 us
    unnamed x19, local copies, waits for them, and re-layouts  5.83 us
    dot_general x1, matrix products, on_device(): jnp.dot(normed, whole_key, preferred_element_type=jnp.float32)  5.18 us
    dot_general x1, matrix products, on_device(): jnp.dot(normed, whole_value, preferred_element_type=jnp.float32)  2.82 us

profile of v4, /device:TPU:0, one launch (start us, length us, event | category | flops | bytes accessed | tf_op | source)
XLA Modules:
  0.0 110.4 jit_solution(15546414848593136417)
XLA Ops:
  0.0 0.0 copy-start
  0.8 0.7 concatenate.12.aux_ref
  1.5 1.6 %copy-done.1 = bf16[1,1024,1024]{2,1,0:T(8,128)(2,1)S(1)} copy-done((bf16[1,1024,1024]{2,1,0:T(8,128)(2,1)S(1)}, bf16[1,1024,1024]{2,1,0:T(8,128)(2,1)}, u32[]{:S(2)}) %copy-start.1) | copy-done | bytes 2097176
  3.1 0.9 copy-done.3
  4.0 0.9 copy-done.4
  5.0 42.7 %shard_map.100 = (bf16[2,1024,1024]{2,1,0:T(8,128)(2,1)}, bf16[1024,1024]{1,0:T(8,128)(2,1)S(1)}, f32[16,128]{1,0:T(8,128)S(1)}, bf16[512,1024]{1,0:T(8,128)(2,1)S(1)}, f32[16,128]{1,0:T(8,128)S(1)}) custom-call(bf16[128,1024]{1,0:T(8,128)(2,1)S(1)} %bitcast.57, bf16[128,1024]{1,0:T(8,128)(2,1)S(1)} %bitcast.58, bf16[1024,1024]{1,0:T(8,128)(2,1)S(1)} %bitcast.54, ...), custom_call_target="tpu_custom_call" | custom-call | tf_op jit(solution)/shard_map/pallas_call | solution.py:248
  47.7 0.0 copy-start.6
  47.7 0.3 convert_reduce_fusion
  48.0 0.7 fusion.3
  48.7 0.5 slice.21
  49.3 0.7 convert_compare_fusion
  49.9 0.0 copy-done.6
  49.9 5.2 %fusion.42 = (bf16[1024]{0:T(1024)(128)(2,1)S(1)}, bf16[1024,1024]{0,1:T(8,128)(2,1)S(1)}) fusion(bf16[2,1024,1024]{2,1,0:T(8,128)(2,1)S(1)} %copy-done.6, bf16[1024,1024]{1,0:T(8,128)(2,1)S(1)} %get-tuple-element.12, f32[1024]{0:T(1024)S(1)} %get-tuple-element.20, f32[1024]{0:T(1024)S(1)} %add_rsqrt_fusion, f32[1024]{0:T(1024)S(1)} %broadcast_multiply_fusion, ...), kind=kOutput, calls=%fused_computation.58 | convolution fusion | flops 2160065536 | bytes 6306816 | tf_op jit(solution)/shard_map/dot_general | solution.py:564
  55.1 2.8 %fusion.24 = bf16[1024,1024]{0,1:T(8,128)(2,1)S(1)} fusion(bf16[2,1024,1024]{2,1,0:T(8,128)(2,1)S(1)} %copy-done.6, bf16[1024,1024]{1,0:T(8,128)(2,1)S(1)} %get-tuple-element.12, f32[1024]{0:T(1024)S(1)} %get-tuple-element.20, f32[1024]{0:T(1024)S(1)} %add_rsqrt_fusion, f32[1024]{0:T(1024)S(1)} %broadcast_multiply_fusion), kind=kOutput, calls=%fused_computation.36 | convolution fusion | flops 2153775104 | bytes 6303744 | tf_op jit(solution)/shard_map/dot_general | solution.py:567
  57.9 0.7 convolution_convert_fusion
  58.7 0.0 copy-start.7
  58.7 23.2 %shard_map.101 = bf16[4,2,4,144,128]{4,3,2,1,0:T(8,128)(2,1)S(1)} custom-call(bf16[2,4,144,128]{3,2,1,0:T(8,128)(2,1)S(1)} %pad_maximum_fusion.part_ref), custom_call_target="tpu_custom_call" | custom-call | tf_op jit(solution)/shard_map/pallas_call | solution.py:384
  81.9 0.2 convert_reduce_fusion.1
  82.2 0.4 fusion.11
  82.6 0.0 copy-done.7
  82.6 1.9 %fusion.17 = bf16[512,1024]{1,0:T(8,128)(2,1)S(1)} fusion(bf16[1024,1024]{1,0:T(8,128)(2,1)S(1)} %copy-done.7, bf16[512,1024]{1,0:T(8,128)(2,1)S(1)} %get-tuple-element.10, f32[1024]{0:T(1024)S(1)} %get-tuple-element.19, f32[512]{0:T(512)S(1)} %add_rsqrt_fusion.2, f32[512]{0:T(512)S(1)} %broadcast_multiply_fusion.2), kind=kOutput, calls=%fused_computation.27 | convolution fusion | flops 1078984704 | bytes 4202496 | tf_op jit(solution)/shard_map/dot_general | solution.py:586
  84.5 0.4 convolution_bitcast_fusion
  84.9 0.3 copy.36
  85.2 1.3 %fusion = bf16[512,8,128]{0,2,1:T(8,128)(2,1)S(1)} fusion(f32[4,512,8]{1,0,2:T(4,128)S(1)} %convolution_bitcast_fusion, bf16[512,8,128,1]{2,1,0,3:T(8,128)(2,1)S(1)} %bitcast.63, bf16[4,8,144,128]{3,2,1,0:T(8,128)(2,1)S(1)} %bitcast.56), kind=kOutput, calls=%fused_computation.3 | convolution fusion | flops 540540928 | bytes 3211264 | tf_op jit(solution)/shard_map/rhk,shkv->srhv/dot_general | solution.py:590
  86.5 0.0 copy-done
  86.5 1.4 %fusion.43 = (f32[512]{0:T(512)S(1)}, f32[512,1024]{1,0:T(8,128)S(1)}) fusion(bf16[512,1024]{0,1:T(8,128)(2,1)S(1)} %bitcast.64, bf16[1024,1024]{1,0:T(8,128)(2,1)S(1)} %copy-done, bf16[512,1024]{1,0:T(8,128)(2,1)S(1)} %get-tuple-element.10), kind=kOutput, calls=%fused_computation.59 | convolution fusion | flops 1075314176 | bytes 6293504 | tf_op jit(solution)/shard_map/dot_general | solution.py:597
  87.9 0.3 multiply_reduce_fusion
  88.3 0.3 copy-done.5
  88.6 0.3 multiply_convert_fusion.centred_ref
  88.9 0.9 copy-done.2
  89.9 19.7 %shard_map.102 = bf16[1024,256]{1,0:T(8,128)(2,1)S(1)} custom-call(bf16[512,1024]{1,0:T(8,128)(2,1)S(1)} %multiply_convert_fusion.centred_ref, f32[512,1024]{1,0:T(8,128)S(1)} %get-tuple-element.18.mixed_ref, bf16[1024,1024]{1,0:T(8,128)(2,1)S(1)} %copy-done.2, bf16[1024,1024]{1,0:T(8,128)(2,1)} %down_ref.1), custom_call_target="tpu_custom_call" | custom-call | tf_op jit(solution)/shard_map/pallas_call | solution.py:503
  109.6 0.8 copy.49
  (16 shorter events, 0.1 us)
Async XLA Ops:
  0.0 86.5 %copy-start = (bf16[1024,1024]{1,0:T(8,128)(2,1)S(1)}, bf16[1024,1024]{1,0:T(8,128)(2,1)}, u32[]{:S(2)}) copy-start(bf16[1024,1024]{1,0:T(8,128)(2,1)} %param.16) | copy-start | bytes 6291460
  1.5 1.6 %copy-start.1 = (bf16[1,1024,1024]{2,1,0:T(8,128)(2,1)S(1)}, bf16[1,1024,1024]{2,1,0:T(8,128)(2,1)}, u32[]{:S(2)}) copy-start(bf16[1,1024,1024]{2,1,0:T(8,128)(2,1)} %param.10) | copy-start | bytes 6291460
  3.1 0.9 copy-start.3
  4.0 0.9 copy-start.4
  47.7 2.3 %copy-start.6 = (bf16[2,1024,1024]{2,1,0:T(8,128)(2,1)S(1)}, bf16[2,1024,1024]{2,1,0:T(8,128)(2,1)}, u32[]{:S(2)}) copy-start(bf16[2,1024,1024]{2,1,0:T(8,128)(2,1)} %get-tuple-element.13) | copy-start | bytes 12582916
  58.7 23.9 %copy-start.7 = (bf16[1024,1024]{1,0:T(8,128)(2,1)S(1)}, bf16[1024,1024]{1,0:T(8,128)(2,1)}, u32[]{:S(2)}) copy-start(bf16[1024,1024]{1,0:T(8,128)(2,1)} %param.15) | copy-start | bytes 6291460
  87.9 0.7 copy-start.5
  88.3 1.6 %copy-start.2 = (bf16[1024,1024]{1,0:T(8,128)(2,1)S(1)}, bf16[1024,1024]{1,0:T(8,128)(2,1)}, u32[]{:S(2)}) copy-start(bf16[1024,1024]{1,0:T(8,128)(2,1)} %up_ref.1) | copy-start | bytes 6291460
